TPU v7x, 512 devices: a whole 4x8x8 slice. The times are simulated.
512 devices in a mesh: dop: 16 (over y, core), rng: 32 (over x, z).
Axes of the slice: x: 4, y: 8, z: 8, core: 2. Of those that a mesh axis runs over, the one named last changes fastest.
Arguments:
- radar_cube: bfloat16 [2, 128, 2048, 512], P(None, 'dop', 'rng'), may hold values from -40 to 40
- train_gates: int32 [16, 1536], P('dop', 'rng'), may hold values from 0 to 63, as said below
- look_angles: int32 [16, 8], P('dop'), may hold values from 0 to 255
Outputs:
- filtered: float32 [2, 16, 8, 2048], P(None, 'dop', None, 'rng')
Inputs may be any that keep to these rules, and one draw needn't show every extreme that they name: `train_gates`: entries k * 48 to (k + 1) * 48 - 1 of a bin's row list in increasing order the gates of the k-th block of 64 consecutive range gates, counted from that block's first gate, that lie outside one run of 16 consecutive gates of the block.
All inputs are finite; a program needn't handle non-finite values.
Results may differ from a plain program's by a relative error of at most 0.014.
The roundings to bfloat16 on the way count: a program that leaves them out, or rounds other values in their place, can miss the bound.
Values may be sent and summed in bfloat16 or wider, within the bound.
A program may use at most 64 MiB of HBM per device.

v0:
```python
import math

import jax
import jax.numpy as jnp
from jax import lax
from jax.sharding import PartitionSpec as P

P_SIZE = 128
NANG = 256
BEAMS = 8


load_eps = 1e-05


def broadcast(block, axis, owner):
    block = jnp.where(lax.axis_index(axis) == owner, block, jnp.zeros_like(block))
    return lax.psum(block, axis)


def doppler_table(bin_count, pulses):
    bin_freq = jnp.arange(bin_count, dtype=jnp.int32) * (pulses // bin_count)
    pulse_index = jnp.arange(pulses, dtype=jnp.int32)
    phase = (bin_freq[:, None] * pulse_index[None, :] % pulses).astype(jnp.float32) * (
        2.0 * math.pi / pulses
    )
    cosine = jnp.cos(phase).astype(jnp.bfloat16)
    sine = jnp.sin(phase).astype(jnp.bfloat16)
    upper = jnp.concatenate([cosine, sine], 1)
    lower = jnp.concatenate([-sine, cosine], 1)
    return jnp.concatenate([upper, lower], 0)


def gram_terms(train_rows):
    real_part = train_rows[0]
    imag_part = train_rows[1]
    contract = (((0,), (0,)), ((), ()))
    stacked = jnp.concatenate([real_part, imag_part], 0)
    power_sum = lax.dot_general(stacked, stacked, contract, preferred_element_type=jnp.float32)
    left_rows = jnp.concatenate([real_part, -imag_part], 0)
    right_rows = jnp.concatenate([imag_part, real_part], 0)
    cross_sum = lax.dot_general(left_rows, right_rows, contract, preferred_element_type=jnp.float32)
    return (power_sum, cross_sum)


def solve_weights(power_sum, cross_sum, look_row, train_count, angle_count):
    channels = power_sum.shape[0]
    top_half = jnp.concatenate([power_sum, cross_sum], 1)
    bottom_half = jnp.concatenate([cross_sum.T, power_sum], 1)
    covariance = jnp.concatenate([top_half, bottom_half], 0) / train_count
    loading = load_eps * jnp.trace(covariance) / (2 * channels)
    covariance = covariance + loading * jnp.eye(2 * channels, dtype=jnp.float32)
    factor = jnp.linalg.cholesky(covariance)
    channel_index = jnp.arange(channels, dtype=jnp.int32)
    slope = 2 * look_row + 1 - angle_count
    modulus = channel_index[:, None] * slope[None, :] % (2 * angle_count)
    phase = modulus.astype(jnp.float32) * (math.pi / angle_count)
    steering = jnp.concatenate([jnp.cos(phase), jnp.sin(phase)], 0)
    whitened = jax.scipy.linalg.solve_triangular(factor, steering, lower=True)
    lengths = jnp.sqrt(jnp.sum(whitened * whitened, axis=0))
    weights = jax.scipy.linalg.solve_triangular(
        factor, whitened / lengths[None, :], trans=1, lower=True
    )
    return weights.astype(jnp.bfloat16)


def filter_gates(spectrum, weights):
    direct = jnp.concatenate([spectrum[0], spectrum[1]], 1)
    rotated = jnp.concatenate([-spectrum[1], spectrum[0]], 1)
    contract = (((0,), (1,)), ((), ()))
    real_out = lax.dot_general(weights, direct, contract, preferred_element_type=jnp.float32)
    imag_out = lax.dot_general(weights, rotated, contract, preferred_element_type=jnp.float32)
    return jnp.stack([real_out, imag_out])


def pack_terms(power_part, cross_part, lower_mask):
    return jnp.where(lower_mask, power_part, cross_part)


def unpack_terms(packed, row_index, col_index):
    lower_mask = row_index >= col_index
    lower_part = jnp.where(lower_mask, packed, 0.0)
    strict_lower = jnp.where(row_index > col_index, packed, 0.0)
    power_sum = lower_part + strict_lower.T
    upper_part = jnp.where(lower_mask, 0.0, packed)
    cross_sum = upper_part - upper_part.T
    return (power_sum, cross_sum)


def on_device(radar_cube, train_gates, look_angles):
    dop_count = lax.axis_size("dop")
    rng_count = lax.axis_size("rng")
    bin_local = train_gates.shape[0]
    bin_count = dop_count * bin_local
    dft_table = doppler_table(bin_count, P_SIZE)
    norm_scale = 1.0 / math.sqrt(P_SIZE)
    segment = lax.all_to_all(radar_cube, "dop", split_axis=2, concat_axis=1, tiled=True)
    flattened = segment.reshape(2 * P_SIZE, -1)
    spectral = (
        jnp.dot(dft_table, flattened, preferred_element_type=jnp.float32) * norm_scale
    ).astype(jnp.bfloat16)
    spectral = spectral.reshape(2, bin_count, segment.shape[2], segment.shape[3])
    binned = lax.all_to_all(spectral, "dop", split_axis=1, concat_axis=2, tiled=True)
    channels = binned.shape[3]
    train_count = train_gates.shape[1] * rng_count
    row_index = lax.broadcasted_iota(jnp.int32, (channels, channels), 0)
    col_index = lax.broadcasted_iota(jnp.int32, (channels, channels), 1)
    lower_mask = row_index >= col_index
    rows = jnp.take(binned[:, 0], train_gates[0], axis=1)
    power_part, cross_part = gram_terms(rows)
    packed_all = jnp.stack([pack_terms(power_part, cross_part, lower_mask)])
    summed = lax.psum(packed_all, "rng")

    def unpack_one(packed):
        return unpack_terms(packed, row_index, col_index)

    power_all, cross_all = jax.vmap(unpack_one)(summed)
    stride = rng_count // bin_local
    rng_index = lax.axis_index("rng")
    lane = lax.axis_index("dop") % stride
    owned = rng_index // stride
    mine = rng_index % stride == lane

    def solve_owned():
        power_one = lax.dynamic_index_in_dim(power_all, owned, 0, keepdims=False)
        cross_one = lax.dynamic_index_in_dim(cross_all, owned, 0, keepdims=False)
        look_one = lax.dynamic_index_in_dim(look_angles, owned, 0, keepdims=False)
        return solve_weights(power_one, cross_one, look_one, train_count, NANG)

    weights_own = lax.cond(
        mine, solve_owned, lambda: jnp.zeros((2 * channels, BEAMS), jnp.bfloat16)
    )
    weight_list = [broadcast(weights_own, "rng", 0 * stride + lane)]
    weights_all = jnp.stack(weight_list)
    outputs = [filter_gates(binned[:, 0], weights_all[0])]
    return jnp.stack(outputs, 1)


def solution(mesh):
    placed = (P(None, "dop", "rng", None), P("dop", "rng"), P("dop", None))
    return jax.shard_map(
        on_device,
        mesh=mesh,
        in_specs=placed,
        out_specs=P(None, "dop", None, "rng"),
        check_vma=False,
    )
```

profile of v0, /device:TPU:8, one launch (start us, length us, event | category | flops | bytes accessed | tf_op | source)
XLA Modules:
  0.0 736.9 jit_solution(393165643155374337)
XLA Ops:
  6.5 0.0 copy-start.2
  6.5 2.8 copy.118
  9.3 9.3 %all-to-all-start = ((bf16[2,8,64,512]{3,1,0,2:T(8,128)(2,1)}), bf16[2,8,64,512]{3,1,0,2:T(8,128)(2,1)S(1)}, u32[]{:S(2)}, u32[]{:S(2)}) async-start(bf16[2,8,64,512]{3,1,0,2:T(8,128)(2,1)} %copy.118), calls=%async_computation | async-start | bytes 2097152 | tf_op jit(solution)/shard_map/all_to_all | solution.py:97
  18.6 0.0 copy-done.2
  18.6 0.1 fusion.131
  18.8 0.1 sine_convert_fusion
  18.9 24.5 %all-to-all-done = bf16[2,8,64,512]{3,1,0,2:T(8,128)(2,1)S(1)} async-done(((bf16[2,8,64,512]{3,1,0,2:T(8,128)(2,1)}), bf16[2,8,64,512]{3,1,0,2:T(8,128)(2,1)S(1)}, u32[]{:S(2)}, u32[]{:S(2)}) %all-to-all-start) | async-done | bytes 1048608 | tf_op jit(solution)/shard_map/all_to_all | solution.py:97
  43.4 0.8 copy.119
  44.2 0.3 copy.135
  44.5 0.3 fusion.103
  44.8 0.1 reshape.210
  44.8 0.7 copy.120
  45.5 6.7 all-to-all-start.1
  52.3 0.0 all-reduce.3.cloned.1.call-start
  52.3 7.3 all-to-all-done.1
  59.6 0.1 copy.121
  59.7 0.8 gather_fusion
  60.5 0.2 fusion.117
  60.7 0.1 fusion.142
  60.9 0.3 fusion.111
  61.2 0.0 copy-start.3
  61.2 1.4 fusion.104
  62.6 0.0 all-reduce.3.cloned.1.call-update
  62.6 0.1 iota_compare_fusion.6
  62.8 0.6 neg.11
  63.4 159.9 %all-reduce.3.cloned.1.call-done = f32[1,512,512]{2,1,0:T(8,128)} async-done(((f32[1,512,512]{2,1,0:T(8,128)}), f32[1,512,512]{2,1,0:T(8,128)}) %all-reduce.3.cloned.1.call-update) | async-done | bytes 1048592 | tf_op jit(solution)/shard_map/psum | solution.py:112
  223.3 0.0 copy-start.1
  223.4 3.1 fusion.138
  226.5 0.0 copy-done.3
  226.5 0.0 copy-done.1
  226.5 0.6 conditional.1
  226.5 0.6 broadcast.446
  227.1 501.2 %psum.15 = bf16[1024,8]{0,1:T(8,128)(2,1)S(1)} all-reduce(bf16[1024,8]{0,1:T(8,128)(2,1)S(1)} %broadcast_select_fusion.2), channel_id=1, replica_groups=mesh['dop'=16,'rng'=32] {'rng'}, use_global_device_ids=true, to_apply=%region_21.22 | all-reduce | flops 8192 | bytes 32768 | tf_op jit(solution)/shard_map/psum | solution.py:18
  728.3 0.1 convolution_bitcast_fusion.1
  728.4 1.0 convolution_bitcast_fusion
  729.4 0.6 maximum_bitcast_fusion
  (10 shorter events, 0.1 us)
Async XLA Ops:
  6.5 12.1 %copy-start.2 = (s32[1,48]{1,0:T(1,128)S(1)}, s32[1,48]{1,0:T(1,128)}, u32[]{:S(2)}) copy-start(s32[1,48]{1,0:T(1,128)} %param.6) | copy-start | bytes 580
  9.3 34.0 %all-to-all-start = ((bf16[2,8,64,512]{3,1,0,2:T(8,128)(2,1)}), bf16[2,8,64,512]{3,1,0,2:T(8,128)(2,1)S(1)}, u32[]{:S(2)}, u32[]{:S(2)}) async-start(bf16[2,8,64,512]{3,1,0,2:T(8,128)(2,1)} %copy.118), calls=%async_computation | async-start | bytes 2097152 | tf_op jit(solution)/shard_map/all_to_all | solution.py:97
  45.5 14.1 %all-to-all-start.1 = ((bf16[2,16,4,512]{3,2,0,1:T(4,128)(2,1)}), bf16[2,16,4,512]{3,2,0,1:T(4,128)(2,1)S(1)}, u32[]{:S(2)}, u32[]{:S(2)}) async-start(bf16[2,16,4,512]{3,2,0,1:T(4,128)(2,1)} %copy.120), calls=%async_computation.1 | async-start | bytes 262144 | tf_op jit(solution)/shard_map/all_to_all | solution.py:103
  52.3 171.1 %all-reduce.3.cloned.1.call-start = ((), (), s32[]{:S(2)}) async-start(), calls=%async_computation.2 | async-start | bytes 2097152 | tf_op jit(solution)/shard_map/psum | solution.py:112
  61.2 165.3 %copy-start.3 = (s32[1,8]{1,0:T(1,128)S(1)}, s32[1,8]{1,0:T(1,128)}, u32[]{:S(2)}) copy-start(s32[1,8]{1,0:T(1,128)} %param.7) | copy-start | bytes 100
  223.3 3.1 copy-start.1
Sparse Core Ops, SparseCore 0:
  62.7 160.5 all-reduce.2
where the time goes:
time: 744 us; the launch traced here: 737 us
  blocking collectives  501 us (67%)
  waiting for transfers between devices  192 us (26%)
  starting transfers between devices  16 us (2%)
  between operations  13.6 us (2%)
    psum x1, blocking collectives, broadcast(): return lax.psum(block, axis)  501 us
    psum x1, waiting for transfers between devices, on_device(): summed = lax.psum(packed_all, 'rng')  160 us
    all_to_all x1, waiting for transfers between devices, on_device(): lax.all_to_all(radar_cube, 'dop', split_axis=2, concat_axis=1, tiled=True)  24.5 us
  transfers between devices with their start and end apart: 3, of which 3 were waited for; matrix products, arithmetic and copies ran while one was open for 0% of the time, Pallas kernels for 0%

commit v1 on v0

v1 whole, which is shorter than its diff:
```python
import functools
import math

import jax
import jax.numpy as jnp
import numpy as np
from jax import lax
from jax.experimental import pallas as pl
from jax.experimental.pallas import tpu as pltpu
from jax.sharding import PartitionSpec as P

F32 = jnp.float32
BF16 = jnp.bfloat16
HIGH = lax.Precision.HIGHEST
MESH = pl.DeviceIdType.MESH
PULSES = 128
NANG = 256
BEAMS = 8
LOAD = 1e-05
DOP = 16
NX = 4
NZ = 8
SIDE = 128


def twiddles():
    angle = 2.0 * math.pi * np.arange(16) / 16
    rounded = lambda v: np.round(v, 12).astype(BF16).astype(np.float32)
    return rounded(np.cos(angle)), rounded(np.sin(angle))


def gather_kernel(cube, gates, full, spec, got, send, even, odd, rows, part, shares,
                  own_sem, a_send, a_recv, b_send, b_recv, x_send, x_recv, r_send, r_recv,
                  z_send, z_recv, f_send, f_recv):
    dop = lax.axis_index("dop")
    rng = lax.axis_index("rng")
    x, z = rng // NZ, lax.rem(rng, NZ)

    def dop_peer(step):
        return {"dop": lax.rem(dop + step, DOP)}

    def x_peer(step):
        return {"rng": lax.rem(x + step, NX) * NZ + z}

    def z_peer(step):
        return {"rng": x * NZ + lax.rem(z + step, NZ)}

    barrier = pltpu.get_barrier_semaphore()

    def greet(peer, count):
        def one(step, carry):
            pl.semaphore_signal(barrier, inc=1, device_id=peer(step), device_id_type=MESH)
            return carry
        lax.fori_loop(1, count, one, 0)

    greet(dop_peer, DOP)
    greet(x_peer, NX)
    greet(z_peer, NZ)
    pl.semaphore_wait(barrier, DOP + NX + NZ - 3)

    def tile_of(index):
        return (pl.ds(pl.multiple_of(index // 4 * 16, 16), 16),
                pl.ds(pl.multiple_of(lax.rem(index, 4) * 128, 128), 128))

    def loop(count, body):
        def one(step, carry):
            body(step)
            return carry
        lax.fori_loop(1, count, one, 0)

    def a_copy(step):
        g, c = tile_of(lax.rem(dop + step, DOP))
        return pltpu.make_async_remote_copy(
            src_ref=cube.at[:, :, g, c], dst_ref=got.at[step], send_sem=a_send.at[step],
            recv_sem=a_recv.at[step], device_id=dop_peer(step), device_id_type=MESH)

    loop(DOP, lambda step: a_copy(step).start())
    g, c = tile_of(dop)
    own = pltpu.make_async_copy(cube.at[:, :, g, c], got.at[0], own_sem)
    own.start()
    own.wait()
    sign = jnp.where(lax.rem(dop, 2) == 0, 1.0, -1.0).astype(F32)
    first = got[0].astype(F32)
    even[...] = first
    odd[...] = sign * first

    def fold(step):
        a_copy(step).wait_recv()
        block = got[step].astype(F32)
        flip = jnp.where(lax.rem(step, 2) == 0, sign, -sign)
        even[...] += block
        odd[...] += flip * block

    loop(DOP, fold)

    cosine, sine = twiddles()
    norm = 1.0 / math.sqrt(PULSES)
    for half in range(2):
        rows8 = slice(8 * half, 8 * half + 8)
        for parity, source in enumerate((even, odd)):
            re = [source[0, q, rows8, :] for q in range(8)]
            im = [source[1, q, rows8, :] for q in range(8)]
            for b in range(parity, DOP, 2):
                up = low = None
                for q in range(8):
                    cb, sb = float(cosine[b * q % 16]), float(sine[b * q % 16])
                    terms_up = [t for t in ((cb, re[q]), (sb, im[q])) if t[0] != 0.0]
                    terms_low = [t for t in ((-sb, re[q]), (cb, im[q])) if t[0] != 0.0]
                    for k, v in terms_up:
                        up = k * v if up is None else up + k * v
                    for k, v in terms_low:
                        low = k * v if low is None else low + k * v
                even_out = (up * norm, low * norm)
                for i in range(2):
                    part[i * 16 + b, rows8, 0:128] = even_out[i]
    for b in range(DOP):
        for i in range(2):
            send[b, i] = part[i * 16 + b, :, 0:128].astype(BF16)

    def b_copy(step):
        return pltpu.make_async_remote_copy(
            src_ref=send.at[lax.rem(dop + step, DOP)], dst_ref=spec.at[:, g, c], send_sem=b_send.at[step],
            recv_sem=b_recv.at[step], device_id=dop_peer(step), device_id_type=MESH)

    loop(DOP, lambda step: b_copy(step).start())
    spec[:, g, c] = send[dop]
    loop(DOP, lambda step: b_copy(step).wait_recv())

    gate = lax.broadcasted_iota(jnp.int32, (64, 48), 0)
    hit = jnp.where(gate == gates[...], 1.0, 0.0)
    mask = jnp.max(hit, axis=1, keepdims=True)
    for i in range(2):
        rows[0, i] = (spec[i].astype(F32) * mask).astype(BF16)

    def x_copy(step):
        return pltpu.make_async_remote_copy(
            src_ref=rows.at[0], dst_ref=rows.at[step], send_sem=x_send.at[step],
            recv_sem=x_recv.at[step], device_id=x_peer(step), device_id_type=MESH)

    loop(NX, lambda step: x_copy(step).start())
    loop(NX, lambda step: x_copy(step).wait_recv())

    def columns(block):
        lanes = pl.ds(pl.multiple_of(block * SIDE, SIDE), SIDE)
        return (rows[:, 0, :, lanes].reshape(256, SIDE), rows[:, 1, :, lanes].reshape(256, SIDE))

    def dot(a, b):
        return lax.dot_general(a, b, (((0,), (0,)), ((), ())), preferred_element_type=F32)

    def power(a, b):
        return dot(a[0], b[0]) + dot(a[1], b[1])

    def cross(a, b):
        return dot(a[0], b[1]) - dot(a[1], b[0])

    near, far = lax.rem(x + 1, NX), lax.rem(x + 2, NX)
    mine = columns(x)
    low1, high1 = columns(jnp.minimum(x, near)), columns(jnp.maximum(x, near))
    low2, high2 = columns(jnp.minimum(x, far)), columns(jnp.maximum(x, far))
    lower = lax.broadcasted_iota(jnp.int32, (SIDE, SIDE), 0) >= lax.broadcasted_iota(jnp.int32, (SIDE, SIDE), 1)
    tiles = (jnp.where(lower, power(mine, mine), cross(mine, mine)), power(low1, high1), cross(low1, high1),
             jnp.where(x < 2, power(low2, high2), cross(low2, high2)))
    for t in range(4):
        for k in range(NZ):
            shares_rows = slice(16 * k, 16 * k + 16)
            part[k, :, 128 * t:128 * t + 128] = tiles[t][shares_rows]

    def r_copy(step):
        return pltpu.make_async_remote_copy(
            src_ref=part.at[lax.rem(z + step, NZ)], dst_ref=shares.at[step], send_sem=r_send.at[step],
            recv_sem=r_recv.at[step], device_id=z_peer(step), device_id_type=MESH)

    loop(NZ, lambda step: r_copy(step).start())
    shares[0] = part[z]

    loop(NZ, lambda step: r_copy(step).wait_recv())
    total = shares[0]
    for step in range(1, NZ):
        total = total + shares[step]
    strip = pl.ds(pl.multiple_of(z * 16, 16), 16)
    full[x, strip, :] = total * (1.0 / 1536.0)

    def z_copy(step):
        return pltpu.make_async_remote_copy(
            src_ref=full.at[x, strip], dst_ref=full.at[x, strip], send_sem=z_send.at[step],
            recv_sem=z_recv.at[step], device_id=z_peer(step), device_id_type=MESH)

    loop(NZ, lambda step: z_copy(step).start())
    loop(NZ, lambda step: z_copy(step).wait_recv())

    def f_copy(step):
        return pltpu.make_async_remote_copy(
            src_ref=full.at[x], dst_ref=full.at[x], send_sem=f_send.at[step],
            recv_sem=f_recv.at[step], device_id=x_peer(step), device_id_type=MESH)

    loop(NX, lambda step: f_copy(step).start())
    loop(NX, lambda step: f_copy(step).wait_recv())

    loop(DOP, lambda step: a_copy(step).wait_send())
    loop(DOP, lambda step: b_copy(step).wait_send())
    loop(NX, lambda step: x_copy(step).wait_send())
    loop(NZ, lambda step: r_copy(step).wait_send())
    loop(NZ, lambda step: z_copy(step).wait_send())
    loop(NX, lambda step: f_copy(step).wait_send())


def gather(cube, gates):
    dma = pltpu.SemaphoreType.DMA
    return pl.pallas_call(
        gather_kernel,
        out_shape=(jax.ShapeDtypeStruct((4, SIDE, 512), F32), jax.ShapeDtypeStruct((2, 64, 512), BF16)),
        in_specs=[pl.BlockSpec(memory_space=pl.ANY), pl.BlockSpec(memory_space=pltpu.VMEM)],
        out_specs=(pl.BlockSpec(memory_space=pltpu.VMEM),) * 2,
        scratch_shapes=[
            pltpu.VMEM((DOP, 2, 8, 16, 128), BF16),
            pltpu.VMEM((DOP, 2, 16, 128), BF16),
            pltpu.VMEM((2, 8, 16, 128), F32),
            pltpu.VMEM((2, 8, 16, 128), F32),
            pltpu.VMEM((NX, 2, 64, 512), BF16),
            pltpu.VMEM((32, 16, 512), F32),
            pltpu.VMEM((NZ, 16, 512), F32),
            dma(()),
            dma((DOP,)), dma((DOP,)), dma((DOP,)), dma((DOP,)), dma((NX,)), dma((NX,)), dma((NZ,)), dma((NZ,)),
            dma((NZ,)), dma((NZ,)), dma((NX,)), dma((NX,)),
        ],
        compiler_params=pltpu.CompilerParams(collective_id=0, has_side_effects=True, vmem_limit_bytes=32 << 20),
        cost_estimate=pl.CostEstimate(flops=10**9, bytes_accessed=10**7, transcendentals=0),
    )(cube, gates)


def parts3(x):
    a = x.astype(BF16).astype(F32)
    r = x - a
    b = r.astype(BF16).astype(F32)
    c = (r - b).astype(BF16).astype(F32)
    return a, b, c

def left6(t):
    a, b, c = t
    return [a, a, b, a, b, c]

def right6(t):
    a, b, c = t
    return [a, b, a, c, b, a]

def neg(t):
    return tuple(-v for v in t)

def invert_block(dr, di):
    lane = lax.broadcasted_iota(jnp.int32, (8, 128), 1)
    sub = lax.broadcasted_iota(jnp.int32, (8, 128), 0)
    wide = lax.broadcasted_iota(jnp.int32, (128, 128), 1)
    for p in range(16):
        o = 8 * p
        rr, ri = dr[o:o+8, :], di[o:o+8, :]
        cr = [jnp.broadcast_to(rr[:, o+j:o+j+1], (8, 128)) for j in range(8)]
        ci = [jnp.broadcast_to(ri[:, o+j:o+j+1], (8, 128)) for j in range(8)]
        inside = (lane >= o) & (lane < o + 8)
        xr = jnp.where(inside, jnp.where(lane == o + sub, 1.0, 0.0), rr)
        xi = jnp.where(inside, 0.0, ri)
        for i in range(8):
            inv = 1.0 / cr[i][i:i+1, :]
            here = sub == i
            def step(vr, vi):
                tr = vr[i:i+1, :] * inv
                ti = vi[i:i+1, :] * inv
                nr = jnp.where(here, tr, vr - (cr[i] * tr - ci[i] * ti))
                ni = jnp.where(here, ti, vi - (cr[i] * ti + ci[i] * tr))
                return nr, ni
            for j in range(i + 1, 8):
                cr[j], ci[j] = step(cr[j], ci[j])
            xr, xi = step(xr, xi)
        sign = jnp.where(lane < o, -1.0, 1.0)
        a, b = parts3(sign * rr), parts3(-sign * ri)
        left = jnp.concatenate(left6(a) + left6(b), 0).astype(BF16)
        u, v = parts3(xr), parts3(xi)
        right = jnp.concatenate([
            jnp.concatenate(right6(u) + right6(neg(v)), 0),
            jnp.concatenate(right6(v) + right6(u), 0)], 1).astype(BF16)
        upd = lax.dot_general(left, right, (((0,), (0,)), ((), ())), preferred_element_type=F32)
        hole = (wide >= o) & (wide < o + 8)
        dr[...] = jnp.where(hole, 0.0, dr[...]) - upd[:, :128]
        di[...] = jnp.where(hole, 0.0, di[...]) - upd[:, 128:]
        dr[o:o+8, :] = xr
        di[o:o+8, :] = xi

def solve_body(tiles_ref, steer_ref, spec_ref, out_ref, dr, di, row, w, x):
    eye = lax.broadcasted_iota(jnp.int32, (128, 128), 0) - lax.broadcasted_iota(jnp.int32, (128, 128), 1)
    tr = 0.0
    for i in range(4):
        tr = tr + jnp.sum(jnp.where(eye == 0, tiles_ref[i, :, 0:128], 0.0))
    load = LOAD * tr / 512.0
    def off(i, j):
        if j - i == 1:
            return (i, 1), (i, 2)
        if j - i == 3:
            return (3, 1), (3, 2)
        return (i, 3), (i + 2, 3)
    for i in range(4):
        for j in range(i + 1, 4):
            (a, b), (c, d) = off(i, j)
            row[i, 0:128, 128*j:128*j+128] = tiles_ref[a, :, 128*b:128*b+128]
            row[i, 128:256, 128*j:128*j+128] = -tiles_ref[c, :, 128*d:128*d+128]
        t = tiles_ref[i, :, 0:128]
        tt = t.T
        row[i, 0:128, 128*i:128*i+128] = jnp.where(eye > 0, t, tt) + jnp.where(eye == 0, load, 0.0)
        row[i, 128:256, 128*i:128*i+128] = jnp.where(eye > 0, tt, jnp.where(eye < 0, -t, 0.0))
        row[i, 0:128, 512:640] = steer_ref[0, 128*i:128*i+128, :]
        row[i, 128:256, 512:640] = steer_ref[1, 128*i:128*i+128, :]

    def body(k, _):
        dr[...] = jnp.zeros_like(dr)
        for kk in range(4):
            @pl.when(k == kk)
            def _():
                dr[...] = row[kk, 0:128, 128*kk:128*kk+128]
                di[...] = row[kk, 128:256, 128*kk:128*kk+128]
        invert_block(dr, di)
        for kk in range(4):
            @pl.when(k == kk)
            def _():
                s = 128 * (kk + 1)
                a, b = dr[...], di[...]
                emb = jnp.concatenate([jnp.concatenate([a, -b], 1), jnp.concatenate([b, a], 1)], 0)
                w[kk, :, s:640] = jnp.dot(emb, row[kk, :, s:640], preferred_element_type=F32, precision=HIGH)
                for i in range(kk + 1, 4):
                    c = 128 * i
                    lhs = row[kk, :, c:c+128]
                    wr = w[kk, 0:128, c:640]
                    wi = w[kk, 128:256, c:640]
                    both = jnp.concatenate([jnp.concatenate([wr, wi], 1), jnp.concatenate([wi, -wr], 1)], 0)
                    n = 640 - c
                    u = lax.dot_general(lhs, both, (((0,), (0,)), ((), ())), preferred_element_type=F32, precision=HIGH)
                    row[i, 0:128, c:640] -= u[:, :n]
                    row[i, 128:256, c:640] -= u[:, n:]
        return 0
    lax.fori_loop(0, 4, body, 0)
    q = jnp.zeros((1, 128), F32)
    for k in (3, 2, 1, 0):
        y = w[k, :, 512:640]
        for j in range(k + 1, 4):
            wr = w[k, 0:128, 128*j:128*j+128]
            wi = w[k, 128:256, 128*j:128*j+128]
            emb = jnp.concatenate([jnp.concatenate([wr, -wi], 1), jnp.concatenate([wi, wr], 1)], 0)
            y = y - jnp.dot(emb, x[j], preferred_element_type=F32, precision=HIGH)
        x[k] = y
        for h in range(2):
            q = q + jnp.sum(y[128*h:128*h+128] * steer_ref[h, 128*k:128*k+128, :], axis=0, keepdims=True)
    lanes = lax.broadcasted_iota(jnp.int32, (1, 128), 1)
    scale = jnp.where(lanes < BEAMS, lax.rsqrt(jnp.where(lanes < BEAMS, q, 1.0)), 0.0)
    re = jnp.zeros((64, 128), F32)
    im = jnp.zeros((64, 128), F32)
    wr = jnp.concatenate([x[k, 0:128] for k in range(4)], 0)
    wi = jnp.concatenate([x[k, 128:256] for k in range(4)], 0)
    wr = (wr * scale).astype(BF16)
    wi = (wi * scale).astype(BF16)
    sr, si = spec_ref[0], spec_ref[1]
    dot = functools.partial(jnp.dot, preferred_element_type=F32)
    re = dot(sr, wr) + dot(si, wi)
    im = dot(sr, wi) - dot(si, wr)
    out_ref[0] = re.T[0:8]
    out_ref[1] = im.T[0:8]

SCR = [pltpu.VMEM((128,128),F32), pltpu.VMEM((128,128),F32), pltpu.VMEM((4,256,640),F32), pltpu.VMEM((4,256,640),F32), pltpu.VMEM((4,256,128),F32)]
def solve(tiles, steer, spec):
    return pl.pallas_call(solve_body, out_shape=jax.ShapeDtypeStruct((2,8,64),F32),
       in_specs=[pl.BlockSpec(memory_space=pltpu.VMEM)]*3, out_specs=pl.BlockSpec(memory_space=pltpu.VMEM),
       scratch_shapes=SCR, compiler_params=pltpu.CompilerParams(vmem_limit_bytes=48<<20))(tiles, steer, spec)


def on_device(radar_cube, train_gates, look_angles):
    full, spec = gather(radar_cube, train_gates)
    channel = jnp.arange(512, dtype=jnp.int32)
    slope = 2 * look_angles[0] + 1 - NANG
    phase = (channel[:, None] * slope[None, :] % (2 * NANG)).astype(F32) * (math.pi / NANG)
    steering = jnp.stack([jnp.cos(phase), jnp.sin(phase)])
    steering = jnp.pad(steering, ((0, 0), (0, 0), (0, 128 - BEAMS)))
    return solve(full, steering, spec)[:, None]


def solution(mesh):
    return jax.shard_map(
        on_device,
        mesh=mesh,
        in_specs=(P(None, "dop", "rng", None), P("dop", "rng"), P("dop", None)),
        out_specs=P(None, "dop", None, "rng"),
        check_vma=False,
    )
```

time: 744 us -> 113 us (0.15)
  the two profiles are of different devices: /device:TPU:8 before, /device:TPU:1 now
where the time goes in v1:
time: 113 us
  Pallas kernels  111 us (98%)
    pallas_call x1, Pallas kernels, gather(): pl.pallas_call(gather_kernel, out_shape=(jax.ShapeDtypeStruct((4, SIDE, 5...  82.7 us
    pallas_call x1, Pallas kernels, solve(): pl.pallas_call(solve_body, out_shape=jax.ShapeDtypeStruct((2, 8, 64), F32...  28.1 us

profile of v1, /device:TPU:1, one launch (start us, length us, event | category | flops | bytes accessed | tf_op | source)
XLA Modules:
  0.0 112.6 jit_solution(13963348623109308473)
XLA Ops:
  0.0 0.0 copy-start
  0.0 0.7 add_bitcast_fusion
  0.8 0.2 fusion.7
  0.9 0.2 copy.5
  1.1 0.0 copy-start.1
  1.2 0.1 copy-done
  1.2 0.6 copy-done.1
  1.8 82.7 %shard_map.37 = (f32[4,128,512]{2,1,0:T(8,128)S(1)}, bf16[2,64,512]{2,1,0:T(8,128)(2,1)S(1)}) custom-call(bf16[2,8,64,512]{3,2,1,0:T(8,128)(2,1)S(1)} %copy-done, s32[1,48]{1,0:T(1,128)S(1)} %copy-done.1), custom_call_target="tpu_custom_call" | custom-call | flops 1000000000 | bytes 10000000 | tf_op jit(solution)/shard_map/pallas_call | solution.py:209
  84.5 28.1 %shard_map.38 = f32[2,8,64]{2,1,0:T(8,128)} custom-call(f32[4,128,512]{2,1,0:T(8,128)S(1)} %get-tuple-element.7.tiles_ref, f32[2,512,128]{2,1,0:T(8,128)S(1)} %pad.4.steer_ref, bf16[2,64,512]{2,1,0:T(8,128)(2,1)S(1)} %get-tuple-element.8.spec_ref), custom_call_target="tpu_custom_call" | custom-call | tf_op jit(solution)/shard_map/pallas_call | solution.py:366
  (2 shorter events, 0.0 us)
Async XLA Ops:
  0.0 1.2 %copy-start = (bf16[2,8,64,512]{3,2,1,0:T(8,128)(2,1)S(1)}, bf16[2,8,64,512]{3,2,1,0:T(8,128)(2,1)}, u32[]{:S(2)}) copy-start(bf16[2,8,64,512]{3,2,1,0:T(8,128)(2,1)} %cube.1) | copy-start | bytes 3145732
  1.1 0.7 copy-start.1

commit v2 on v0

v2 whole, which is shorter than its diff:
```python
import functools
import math

import jax
import jax.numpy as jnp
import numpy as np
from jax import lax
from jax.experimental import pallas as pl
from jax.experimental.pallas import tpu as pltpu
from jax.sharding import PartitionSpec as P

F32 = jnp.float32
BF16 = jnp.bfloat16
HIGH = lax.Precision.HIGHEST
MESH = pl.DeviceIdType.MESH
PULSES = 128
NANG = 256
BEAMS = 8
LOAD = 1e-05
DOP = 16
NX = 4
NZ = 8
RNG = NX * NZ
SIDE = 128
TRAIN = 1536
ROOTS = (0, 20)


def twiddles():
    angle = 2.0 * math.pi * np.arange(16) / 16
    rounded = lambda v: np.round(v, 12).astype(BF16).astype(np.float32)
    return rounded(np.cos(angle)), rounded(np.sin(angle))


def parts3(x):
    a = x.astype(BF16).astype(F32)
    r = x - a
    b = r.astype(BF16).astype(F32)
    c = (r - b).astype(BF16).astype(F32)
    return a, b, c

def left6(t):
    a, b, c = t
    return [a, a, b, a, b, c]

def right6(t):
    a, b, c = t
    return [a, b, a, c, b, a]

def neg(t):
    return tuple(-v for v in t)

def invert_block(dr, di):
    lane = lax.broadcasted_iota(jnp.int32, (8, 128), 1)
    sub = lax.broadcasted_iota(jnp.int32, (8, 128), 0)
    wide = lax.broadcasted_iota(jnp.int32, (128, 128), 1)
    for p in range(16):
        o = 8 * p
        rr, ri = dr[o:o+8, :], di[o:o+8, :]
        cr = [jnp.broadcast_to(rr[:, o+j:o+j+1], (8, 128)) for j in range(8)]
        ci = [jnp.broadcast_to(ri[:, o+j:o+j+1], (8, 128)) for j in range(8)]
        inside = (lane >= o) & (lane < o + 8)
        xr = jnp.where(inside, jnp.where(lane == o + sub, 1.0, 0.0), rr)
        xi = jnp.where(inside, 0.0, ri)
        for i in range(8):
            inv = 1.0 / cr[i][i:i+1, :]
            here = sub == i
            def step(vr, vi):
                tr = vr[i:i+1, :] * inv
                ti = vi[i:i+1, :] * inv
                nr = jnp.where(here, tr, vr - (cr[i] * tr - ci[i] * ti))
                ni = jnp.where(here, ti, vi - (cr[i] * ti + ci[i] * tr))
                return nr, ni
            for j in range(i + 1, 8):
                cr[j], ci[j] = step(cr[j], ci[j])
            xr, xi = step(xr, xi)
        sign = jnp.where(lane < o, -1.0, 1.0)
        a, b = parts3(sign * rr), parts3(-sign * ri)
        left = jnp.concatenate(left6(a) + left6(b), 0).astype(BF16)
        u, v = parts3(xr), parts3(xi)
        right = jnp.concatenate([
            jnp.concatenate(right6(u) + right6(neg(v)), 0),
            jnp.concatenate(right6(v) + right6(u), 0)], 1).astype(BF16)
        upd = lax.dot_general(left, right, (((0,), (0,)), ((), ())), preferred_element_type=F32)
        hole = (wide >= o) & (wide < o + 8)
        dr[...] = jnp.where(hole, 0.0, dr[...]) - upd[:, :128]
        di[...] = jnp.where(hole, 0.0, di[...]) - upd[:, 128:]
        dr[o:o+8, :] = xr
        di[o:o+8, :] = xi


def beam_kernel(cube, gates, looks, out, got, send, even, odd, raw, spec, rows, part_d, part_r, share_d, share_r,
                sum_d, sum_r, full, look, steer, dr, di, row, w, x_ref, weights,
                own_sem, a_send, a_recv, b_send, b_recv, x_send, x_recv, rd_send, rd_recv, rr_send, rr_recv,
                gd_send, gd_recv, gr_send, gr_recv, w_send, w_recv):
    dop = lax.axis_index("dop")
    rng = lax.axis_index("rng")
    x, z = rng // NZ, lax.rem(rng, NZ)
    root = jnp.where(lax.rem(dop, 2) == 0, ROOTS[0], ROOTS[1])
    is_root = rng == root

    def dop_peer(step):
        return {"dop": lax.rem(dop + step, DOP)}

    def x_peer(step):
        return {"rng": lax.rem(x + step, NX) * NZ + z}

    def z_peer(step):
        return {"rng": x * NZ + lax.rem(z + step, NZ)}

    def loop(count, body, start=1):
        def one(step, carry):
            body(step)
            return carry
        lax.fori_loop(start, count, one, 0)

    def far_first(count, body):
        def one(k):
            j = count - k
            body(jnp.where(lax.rem(j, 2) == 1, (j + 1) // 2, count - j // 2))
        loop(count, one)

    def others(body):
        def one(r):
            @pl.when(r != rng)
            def _():
                body(r)
        loop(RNG, one, 0)

    barrier = pltpu.get_barrier_semaphore()

    def greet(peer):
        pl.semaphore_signal(barrier, inc=1, device_id=peer, device_id_type=MESH)

    loop(DOP, lambda step: greet(dop_peer(step)))
    loop(RNG, lambda step: greet({"rng": lax.rem(rng + step, RNG)}))
    pl.semaphore_wait(barrier, DOP + RNG - 2)

    def tile_of(index):
        return (pl.ds(pl.multiple_of(index // 4 * 16, 16), 16),
                pl.ds(pl.multiple_of(lax.rem(index, 4) * 128, 128), 128))

    def a_copy(step):
        g, c = tile_of(lax.rem(dop + step, DOP))
        return pltpu.make_async_remote_copy(
            src_ref=cube.at[:, :, g, c], dst_ref=got.at[step], send_sem=a_send.at[step],
            recv_sem=a_recv.at[step], device_id=dop_peer(step), device_id_type=MESH)

    far_first(DOP, lambda step: a_copy(step).start())
    g, c = tile_of(dop)
    own = pltpu.make_async_copy(cube.at[:, :, g, c], got.at[0], own_sem)
    own.start()

    look[...] = jnp.zeros_like(look)
    look[:, 0:BEAMS] = looks[...]
    slope = 2 * look[...] + 1 - NANG
    lanes = lax.broadcasted_iota(jnp.int32, (128, 128), 1)
    for k in range(4):
        channel = lax.broadcasted_iota(jnp.int32, (128, 128), 0) + 128 * k
        turn = (channel * slope) & (2 * NANG - 1)
        phase = turn.astype(F32) * (math.pi / NANG)
        steer[0, 128*k:128*k+128, :] = jnp.where(lanes < BEAMS, jnp.cos(phase), 0.0)
        steer[1, 128*k:128*k+128, :] = jnp.where(lanes < BEAMS, jnp.sin(phase), 0.0)
    gate = lax.broadcasted_iota(jnp.int32, (64, 48), 0)
    mask = jnp.max(jnp.where(gate == gates[...], 1.0, 0.0), axis=1, keepdims=True)

    own.wait()
    sign = jnp.where(lax.rem(dop, 2) == 0, 1.0, -1.0).astype(F32)
    first = got[0].astype(F32)
    even[...] = first
    odd[...] = sign * first

    def fold(step):
        a_copy(step).wait_recv()
        block = got[step].astype(F32)
        flip = jnp.where(lax.rem(step, 2) == 0, sign, -sign)
        even[...] += block
        odd[...] += flip * block

    loop(DOP, fold)

    cosine, sine = twiddles()
    norm = 1.0 / math.sqrt(PULSES)
    for half in range(2):
        rows8 = slice(8 * half, 8 * half + 8)
        for parity, source in enumerate((even, odd)):
            re = [source[0, q, rows8, :] for q in range(8)]
            im = [source[1, q, rows8, :] for q in range(8)]
            for b in range(parity, DOP, 2):
                up = low = None
                for q in range(8):
                    cb, sb = float(cosine[b * q % 16]), float(sine[b * q % 16])
                    for k, v in ((cb, re[q]), (sb, im[q])):
                        if k != 0.0:
                            up = k * v if up is None else up + k * v
                    for k, v in ((-sb, re[q]), (cb, im[q])):
                        if k != 0.0:
                            low = k * v if low is None else low + k * v
                raw[b, 0, rows8, :] = up * norm
                raw[b, 1, rows8, :] = low * norm
    for b in range(DOP):
        send[b] = raw[b].astype(BF16)

    def b_copy(step):
        return pltpu.make_async_remote_copy(
            src_ref=send.at[lax.rem(dop + step, DOP)], dst_ref=spec.at[:, g, c], send_sem=b_send.at[step],
            recv_sem=b_recv.at[step], device_id=dop_peer(step), device_id_type=MESH)

    far_first(DOP, lambda step: b_copy(step).start())
    spec[:, g, c] = send[dop]
    loop(DOP, lambda step: b_copy(step).wait_recv())

    for i in range(2):
        rows[0, i] = (spec[i].astype(F32) * mask).astype(BF16)

    def x_copy(step):
        return pltpu.make_async_remote_copy(
            src_ref=rows.at[0], dst_ref=rows.at[step], send_sem=x_send.at[step],
            recv_sem=x_recv.at[step], device_id=x_peer(step), device_id_type=MESH)

    far_first(NX, lambda step: x_copy(step).start())
    loop(NX, lambda step: x_copy(step).wait_recv())

    def columns(block):
        at = pl.ds(pl.multiple_of(block * SIDE, SIDE), SIDE)
        return (rows[:, 0, :, at].reshape(256, SIDE), rows[:, 1, :, at].reshape(256, SIDE))

    def dot(a, b):
        return lax.dot_general(a, b, (((0,), (0,)), ((), ())), preferred_element_type=F32)

    def power(a, b):
        return dot(a[0], b[0]) + dot(a[1], b[1])

    def cross(a, b):
        return dot(a[0], b[1]) - dot(a[1], b[0])

    def r_copy(part, share, sends, recvs, step):
        return pltpu.make_async_remote_copy(
            src_ref=part.at[lax.rem(z + step, NZ)], dst_ref=share.at[step], send_sem=sends.at[step],
            recv_sem=recvs.at[step], device_id=z_peer(step), device_id_type=MESH)

    rd_copy = functools.partial(r_copy, part_d, share_d, rd_send, rd_recv)
    rr_copy = functools.partial(r_copy, part_r, share_r, rr_send, rr_recv)
    mine = columns(x)
    eye = lax.broadcasted_iota(jnp.int32, (SIDE, SIDE), 0) - lax.broadcasted_iota(jnp.int32, (SIDE, SIDE), 1)
    part_d[...] = jnp.where(eye >= 0, power(mine, mine), cross(mine, mine)).reshape(NZ, 16, SIDE)
    far_first(NZ, lambda step: rd_copy(step).start())
    near, far = lax.rem(x + 1, NX), lax.rem(x + 2, NX)
    low1, high1 = columns(jnp.minimum(x, near)), columns(jnp.maximum(x, near))
    low2, high2 = columns(jnp.minimum(x, far)), columns(jnp.maximum(x, far))
    part_r[:, :, 0:128] = power(low1, high1).reshape(NZ, 16, SIDE)
    part_r[:, :, 128:256] = cross(low1, high1).reshape(NZ, 16, SIDE)
    part_r[:, :, 256:384] = jnp.where(x < 2, power(low2, high2), cross(low2, high2)).reshape(NZ, 16, SIDE)
    far_first(NZ, lambda step: rr_copy(step).start())

    strip = pl.ds(pl.multiple_of(z * 16, 16), 16)

    def strip_of(r, at):
        return full.at[r // NZ, pl.ds(pl.multiple_of(lax.rem(r, NZ) * 16, 16), 16), at]

    def gd_copy(r, target):
        return pltpu.make_async_remote_copy(
            src_ref=sum_d, dst_ref=strip_of(r, slice(0, 128)), send_sem=gd_send, recv_sem=gd_recv.at[r],
            device_id={"rng": target}, device_id_type=MESH)

    def gr_copy(r, target):
        return pltpu.make_async_remote_copy(
            src_ref=sum_r, dst_ref=strip_of(r, slice(128, 512)), send_sem=gr_send, recv_sem=gr_recv.at[r],
            device_id={"rng": target}, device_id_type=MESH)

    def total(part, share, copy):
        loop(NZ, lambda step: copy(step).wait_recv())
        value = part[z]
        for step in range(1, NZ):
            value = value + share[step]
        return value * (1.0 / TRAIN)

    value_d = total(part_d, share_d, rd_copy)

    @pl.when(jnp.logical_not(is_root))
    def _():
        sum_d[...] = value_d
        gd_copy(rng, root).start()
        sum_r[...] = total(part_r, share_r, rr_copy)
        gr_copy(rng, root).start()

    def w_copy(r):
        return pltpu.make_async_remote_copy(
            src_ref=weights, dst_ref=weights, send_sem=w_send.at[r], recv_sem=w_recv,
            device_id={"rng": r}, device_id_type=MESH)

    @pl.when(is_root)
    def _():
        full[x, strip, 0:128] = value_d
        others(lambda r: gd_copy(r, root).wait_recv())
        trace = jnp.zeros((), F32)
        for i in range(4):
            trace = trace + jnp.sum(jnp.where(eye == 0, full[i, :, 0:128], 0.0))
        load = LOAD * trace / 512.0
        for i in range(4):
            t = full[i, :, 0:128]
            tt = t.T
            row[i, 0:128, 128*i:128*i+128] = jnp.where(eye > 0, t, tt) + jnp.where(eye == 0, load, 0.0)
            row[i, 128:256, 128*i:128*i+128] = jnp.where(eye > 0, tt, jnp.where(eye < 0, -t, 0.0))
            row[i, 0:128, 512:640] = steer[0, 128*i:128*i+128, :]
            row[i, 128:256, 512:640] = steer[1, 128*i:128*i+128, :]

        def rest():
            full[x, strip, 128:512] = total(part_r, share_r, rr_copy)
            others(lambda r: gr_copy(r, root).wait_recv())
            for i in range(4):
                for j in range(i + 1, 4):
                    (a, b), (e, d) = place(i, j)
                    row[i, 0:128, 128*j:128*j+128] = full[a, :, 128*b:128*b+128]
                    row[i, 128:256, 128*j:128*j+128] = -full[e, :, 128*d:128*d+128]

        solve(rest, steer, row, w, x_ref, dr, di, weights)
        others(lambda r: w_copy(r).start())

    @pl.when(jnp.logical_not(is_root))
    def _():
        w_copy(root).wait_recv()

    across = (((1,), (1,)), ((), ()))
    with_re = lax.dot_general(weights[...], spec[0], across, preferred_element_type=F32)
    with_im = lax.dot_general(weights[...], spec[1], across, preferred_element_type=F32)
    out[0] = with_re[0:8] + with_im[8:16]
    out[1] = with_re[8:16] - with_im[0:8]

    @pl.when(is_root)
    def _():
        others(lambda r: w_copy(r).wait_send())

    @pl.when(jnp.logical_not(is_root))
    def _():
        gd_copy(rng, root).wait_send()
        gr_copy(rng, root).wait_send()

    loop(DOP, lambda step: a_copy(step).wait_send())
    loop(DOP, lambda step: b_copy(step).wait_send())
    loop(NX, lambda step: x_copy(step).wait_send())
    loop(NZ, lambda step: rd_copy(step).wait_send())
    loop(NZ, lambda step: rr_copy(step).wait_send())


def place(i, j):
    if j - i == 1:
        return (i, 1), (i, 2)
    if j - i == 3:
        return (3, 1), (3, 2)
    return (i, 3), (i + 2, 3)


def solve(rest, steer, row, w, x, dr, di, weights):
    def body(k, carry):
        for kk in range(4):
            @pl.when(k == kk)
            def _():
                dr[...] = row[kk, 0:128, 128*kk:128*kk+128]
                di[...] = row[kk, 128:256, 128*kk:128*kk+128]
        invert_block(dr, di)
        for kk in range(4):
            @pl.when(k == kk)
            def _():
                if kk == 0:
                    rest()
                s = 128 * (kk + 1)
                a, b = dr[...], di[...]
                emb = jnp.concatenate([jnp.concatenate([a, -b], 1), jnp.concatenate([b, a], 1)], 0)
                w[kk, :, s:640] = jnp.dot(emb, row[kk, :, s:640], preferred_element_type=F32, precision=HIGH)
                for i in range(kk + 1, 4):
                    c = 128 * i
                    lhs = row[kk, :, c:c+128]
                    wr = w[kk, 0:128, c:640]
                    wi = w[kk, 128:256, c:640]
                    both = jnp.concatenate([jnp.concatenate([wr, wi], 1), jnp.concatenate([wi, -wr], 1)], 0)
                    n = 640 - c
                    u = lax.dot_general(lhs, both, (((0,), (0,)), ((), ())), preferred_element_type=F32, precision=HIGH)
                    row[i, 0:128, c:640] -= u[:, :n]
                    row[i, 128:256, c:640] -= u[:, n:]
        return carry

    lax.fori_loop(0, 4, body, 0)
    q = jnp.zeros((1, 128), F32)
    for k in (3, 2, 1, 0):
        y = w[k, :, 512:640]
        for j in range(k + 1, 4):
            wr = w[k, 0:128, 128*j:128*j+128]
            wi = w[k, 128:256, 128*j:128*j+128]
            emb = jnp.concatenate([jnp.concatenate([wr, -wi], 1), jnp.concatenate([wi, wr], 1)], 0)
            y = y - jnp.dot(emb, x[j], preferred_element_type=F32, precision=HIGH)
        x[k] = y
        for h in range(2):
            q = q + jnp.sum(y[128*h:128*h+128] * steer[h, 128*k:128*k+128, :], axis=0, keepdims=True)
    lanes = lax.broadcasted_iota(jnp.int32, (1, 128), 1)
    scale = lax.rsqrt(jnp.where(lanes < BEAMS, q, 1.0))
    for k in range(4):
        both = [(x[k, 128*h:128*h+128] * scale).T[0:8] for h in range(2)]
        weights[:, 128*k:128*k+128] = jnp.concatenate(both, 0).astype(BF16)


def beams(cube, gates, looks):
    dma = pltpu.SemaphoreType.DMA
    return pl.pallas_call(
        beam_kernel,
        out_shape=jax.ShapeDtypeStruct((2, BEAMS, 64), F32),
        in_specs=[pl.BlockSpec(memory_space=pl.ANY), pl.BlockSpec(memory_space=pltpu.VMEM),
                  pl.BlockSpec(memory_space=pltpu.VMEM)],
        out_specs=pl.BlockSpec(memory_space=pltpu.VMEM),
        scratch_shapes=[
            pltpu.VMEM((DOP, 2, 8, 16, 128), BF16),
            pltpu.VMEM((DOP, 2, 16, 128), BF16),
            pltpu.VMEM((2, 8, 16, 128), F32),
            pltpu.VMEM((2, 8, 16, 128), F32),
            pltpu.VMEM((DOP, 2, 16, 128), F32),
            pltpu.VMEM((2, 64, 512), BF16),
            pltpu.VMEM((NX, 2, 64, 512), BF16),
            pltpu.VMEM((NZ, 16, 128), F32),
            pltpu.VMEM((NZ, 16, 384), F32),
            pltpu.VMEM((NZ, 16, 128), F32),
            pltpu.VMEM((NZ, 16, 384), F32),
            pltpu.VMEM((16, 128), F32),
            pltpu.VMEM((16, 384), F32),
            pltpu.VMEM((4, SIDE, 512), F32),
            pltpu.VMEM((1, 128), jnp.int32),
            pltpu.VMEM((2, 512, 128), F32),
            pltpu.VMEM((128, 128), F32),
            pltpu.VMEM((128, 128), F32),
            pltpu.VMEM((4, 256, 640), F32),
            pltpu.VMEM((4, 256, 640), F32),
            pltpu.VMEM((4, 256, 128), F32),
            pltpu.VMEM((16, 512), BF16),
            dma(()),
            dma((DOP,)), dma((DOP,)), dma((DOP,)), dma((DOP,)), dma((NX,)), dma((NX,)),
            dma((NZ,)), dma((NZ,)), dma((NZ,)), dma((NZ,)),
            dma(()), dma((RNG,)), dma(()), dma((RNG,)), dma((RNG,)), dma(()),
        ],
        compiler_params=pltpu.CompilerParams(collective_id=0, has_side_effects=True, vmem_limit_bytes=48 << 20),
        cost_estimate=pl.CostEstimate(flops=10**9, bytes_accessed=10**7, transcendentals=0),
    )(cube, gates, looks)


def on_device(radar_cube, train_gates, look_angles):
    return beams(radar_cube, train_gates, look_angles)[:, None]


def solution(mesh):
    return jax.shard_map(
        on_device,
        mesh=mesh,
        in_specs=(P(None, "dop", "rng", None), P("dop", "rng"), P("dop", None)),
        out_specs=P(None, "dop", None, "rng"),
        check_vma=False,
    )
```

time: 744 us -> 102 us (0.14)
  the two profiles are of different devices: /device:TPU:8 before, /device:TPU:1 now
where the time goes in v2:
time: 102 us
  Pallas kernels  99.1 us (97%)
  local copies, waits for them, and re-layouts  3.13 us (3%)
    pallas_call x1, Pallas kernels, beams(): pl.pallas_call(beam_kernel, out_shape=jax.ShapeDtypeStruct((2, BEAMS, 64)...  99.1 us
    unnamed x7, local copies, waits for them, and re-layouts  3.13 us

profile of v2, /device:TPU:1, one launch (start us, length us, event | category | flops | bytes accessed | tf_op | source)
XLA Modules:
  0.0 102.2 jit_solution(3617369572183121262)
XLA Ops:
  0.0 0.0 copy-start
  0.0 1.2 %copy-done = bf16[2,8,64,512]{3,2,1,0:T(8,128)(2,1)S(1)} copy-done((bf16[2,8,64,512]{3,2,1,0:T(8,128)(2,1)S(1)}, bf16[2,8,64,512]{3,2,1,0:T(8,128)(2,1)}, u32[]{:S(2)}) %copy-start) | copy-done | bytes 1048600
  1.2 0.0 copy-start.1
  1.2 0.7 copy-done.1
  1.9 0.0 copy-start.2
  1.9 0.7 copy-done.2
  2.5 99.1 %shard_map.37 = f32[2,8,64]{2,1,0:T(8,128)S(1)} custom-call(bf16[2,8,64,512]{3,2,1,0:T(8,128)(2,1)S(1)} %copy-done, s32[1,48]{1,0:T(1,128)S(1)} %copy-done.1, s32[1,8]{1,0:T(1,128)S(1)} %copy-done.2), custom_call_target="tpu_custom_call" | custom-call | flops 1000000000 | bytes 10000000 | tf_op jit(solution)/shard_map/pallas_call | solution.py:404
  101.6 0.6 copy.6
Async XLA Ops:
  0.0 1.2 %copy-start = (bf16[2,8,64,512]{3,2,1,0:T(8,128)(2,1)S(1)}, bf16[2,8,64,512]{3,2,1,0:T(8,128)(2,1)}, u32[]{:S(2)}) copy-start(bf16[2,8,64,512]{3,2,1,0:T(8,128)(2,1)} %cube.1) | copy-start | bytes 3145732
  1.2 0.7 copy-start.1
  1.9 0.7 copy-start.2

commit v3 on v2

--- a/solution.py
+++ b/solution.py
@@ -22,6 +22,7 @@
 NZ = 8
 RNG = NX * NZ
 SIDE = 128
+TR = 48
 TRAIN = 1536
 ROOTS = (0, 20)
 
@@ -54,26 +55,44 @@
     lane = lax.broadcasted_iota(jnp.int32, (8, 128), 1)
     sub = lax.broadcasted_iota(jnp.int32, (8, 128), 0)
     wide = lax.broadcasted_iota(jnp.int32, (128, 128), 1)
+
+    def spread(v, o):
+        return [jnp.broadcast_to(v[:, o+j:o+j+1], (8, 128)) for j in range(8)]
+
+    rr, ri = dr[0:8, :], di[0:8, :]
     for p in range(16):
         o = 8 * p
-        rr, ri = dr[o:o+8, :], di[o:o+8, :]
-        cr = [jnp.broadcast_to(rr[:, o+j:o+j+1], (8, 128)) for j in range(8)]
-        ci = [jnp.broadcast_to(ri[:, o+j:o+j+1], (8, 128)) for j in range(8)]
+        cr, ci = spread(rr, o), spread(ri, o)
         inside = (lane >= o) & (lane < o + 8)
         xr = jnp.where(inside, jnp.where(lane == o + sub, 1.0, 0.0), rr)
         xi = jnp.where(inside, 0.0, ri)
         for i in range(8):
             inv = 1.0 / cr[i][i:i+1, :]
             here = sub == i
+
             def step(vr, vi):
                 tr = vr[i:i+1, :] * inv
                 ti = vi[i:i+1, :] * inv
                 nr = jnp.where(here, tr, vr - (cr[i] * tr - ci[i] * ti))
                 ni = jnp.where(here, ti, vi - (cr[i] * ti + ci[i] * tr))
                 return nr, ni
+
             for j in range(i + 1, 8):
                 cr[j], ci[j] = step(cr[j], ci[j])
             xr, xi = step(xr, xi)
+        if p < 15:
+            br, bi = dr[o+8:o+16, :], di[o+8:o+16, :]
+            er, ei = spread(br, o), spread(bi, o)
+            ar, ai = [], []
+            for j in range(8):
+                tr, ti = xr[j:j+1, :], xi[j:j+1, :]
+                ar.append(er[j] * tr - ei[j] * ti)
+                ai.append(er[j] * ti + ei[j] * tr)
+            while len(ar) > 1:
+                ar = [a + b for a, b in zip(ar[::2], ar[1::2])]
+                ai = [a + b for a, b in zip(ai[::2], ai[1::2])]
+            ahead_r = jnp.where(inside, 0.0, br) - ar[0]
+            ahead_i = jnp.where(inside, 0.0, bi) - ai[0]
         sign = jnp.where(lane < o, -1.0, 1.0)
         a, b = parts3(sign * rr), parts3(-sign * ri)
         left = jnp.concatenate(left6(a) + left6(b), 0).astype(BF16)
@@ -87,10 +106,12 @@
         di[...] = jnp.where(hole, 0.0, di[...]) - upd[:, 128:]
         dr[o:o+8, :] = xr
         di[o:o+8, :] = xi
-
-
-def beam_kernel(cube, gates, looks, out, got, send, even, odd, raw, spec, rows, part_d, part_r, share_d, share_r,
-                sum_d, sum_r, full, look, steer, dr, di, row, w, x_ref, weights,
+        if p < 15:
+            rr, ri = ahead_r, ahead_i
+
+
+def beam_kernel(cube, indices, out, got, send, even, odd, raw, spec, rows, part_d, part_r, share_d, share_r,
+                sum_d, sum_r, full, steer, dr, di, row, w, x_ref, weights,
                 own_sem, a_send, a_recv, b_send, b_recv, x_send, x_recv, rd_send, rd_recv, rr_send, rr_recv,
                 gd_send, gd_recv, gr_send, gr_recv, w_send, w_recv):
     dop = lax.axis_index("dop")
@@ -133,8 +154,23 @@
         pl.semaphore_signal(barrier, inc=1, device_id=peer, device_id_type=MESH)
 
     loop(DOP, lambda step: greet(dop_peer(step)))
-    loop(RNG, lambda step: greet({"rng": lax.rem(rng + step, RNG)}))
-    pl.semaphore_wait(barrier, DOP + RNG - 2)
+    aside = (root // NZ != x) & (lax.rem(root, NZ) != z)
+
+    @pl.when(is_root)
+    def _():
+        loop(RNG, lambda step: greet({"rng": lax.rem(rng + step, RNG)}))
+
+    @pl.when(jnp.logical_not(is_root))
+    def _():
+        loop(NX, lambda step: greet(x_peer(step)))
+        loop(NZ, lambda step: greet(z_peer(step)))
+
+    @pl.when(aside)
+    def _():
+        greet({"rng": root})
+
+    near_count = DOP + NX + NZ - 3
+    pl.semaphore_wait(barrier, jnp.where(is_root, DOP + RNG - 2, jnp.where(aside, near_count + 1, near_count)))
 
     def tile_of(index):
         return (pl.ds(pl.multiple_of(index // 4 * 16, 16), 16),
@@ -151,9 +187,7 @@
     own = pltpu.make_async_copy(cube.at[:, :, g, c], got.at[0], own_sem)
     own.start()
 
-    look[...] = jnp.zeros_like(look)
-    look[:, 0:BEAMS] = looks[...]
-    slope = 2 * look[...] + 1 - NANG
+    slope = 2 * indices[1:2] + 1 - NANG
     lanes = lax.broadcasted_iota(jnp.int32, (128, 128), 1)
     for k in range(4):
         channel = lax.broadcasted_iota(jnp.int32, (128, 128), 0) + 128 * k
@@ -161,8 +195,8 @@
         phase = turn.astype(F32) * (math.pi / NANG)
         steer[0, 128*k:128*k+128, :] = jnp.where(lanes < BEAMS, jnp.cos(phase), 0.0)
         steer[1, 128*k:128*k+128, :] = jnp.where(lanes < BEAMS, jnp.sin(phase), 0.0)
-    gate = lax.broadcasted_iota(jnp.int32, (64, 48), 0)
-    mask = jnp.max(jnp.where(gate == gates[...], 1.0, 0.0), axis=1, keepdims=True)
+    gate = lax.broadcasted_iota(jnp.int32, (64, TR), 0)
+    pick = jnp.where(gate == indices[0:1, 0:TR], 1.0, 0.0).astype(BF16)
 
     own.wait()
     sign = jnp.where(lax.rem(dop, 2) == 0, 1.0, -1.0).astype(F32)
@@ -211,7 +245,8 @@
     loop(DOP, lambda step: b_copy(step).wait_recv())
 
     for i in range(2):
-        rows[0, i] = (spec[i].astype(F32) * mask).astype(BF16)
+        rows[0, i] = lax.dot_general(
+            pick, spec[i], (((0,), (0,)), ((), ())), preferred_element_type=F32).astype(BF16)
 
     def x_copy(step):
         return pltpu.make_async_remote_copy(
@@ -223,7 +258,7 @@
 
     def columns(block):
         at = pl.ds(pl.multiple_of(block * SIDE, SIDE), SIDE)
-        return (rows[:, 0, :, at].reshape(256, SIDE), rows[:, 1, :, at].reshape(256, SIDE))
+        return (rows[:, 0, :, at].reshape(NX * TR, SIDE), rows[:, 1, :, at].reshape(NX * TR, SIDE))
 
     def dot(a, b):
         return lax.dot_general(a, b, (((0,), (0,)), ((), ())), preferred_element_type=F32)
@@ -399,13 +434,12 @@
         weights[:, 128*k:128*k+128] = jnp.concatenate(both, 0).astype(BF16)
 
 
-def beams(cube, gates, looks):
+def beams(cube, indices):
     dma = pltpu.SemaphoreType.DMA
     return pl.pallas_call(
         beam_kernel,
         out_shape=jax.ShapeDtypeStruct((2, BEAMS, 64), F32),
-        in_specs=[pl.BlockSpec(memory_space=pl.ANY), pl.BlockSpec(memory_space=pltpu.VMEM),
-                  pl.BlockSpec(memory_space=pltpu.VMEM)],
+        in_specs=[pl.BlockSpec(memory_space=pl.ANY), pl.BlockSpec(memory_space=pltpu.VMEM)],
         out_specs=pl.BlockSpec(memory_space=pltpu.VMEM),
         scratch_shapes=[
             pltpu.VMEM((DOP, 2, 8, 16, 128), BF16),
@@ -414,7 +448,7 @@
             pltpu.VMEM((2, 8, 16, 128), F32),
             pltpu.VMEM((DOP, 2, 16, 128), F32),
             pltpu.VMEM((2, 64, 512), BF16),
-            pltpu.VMEM((NX, 2, 64, 512), BF16),
+            pltpu.VMEM((NX, 2, TR, 512), BF16),
             pltpu.VMEM((NZ, 16, 128), F32),
             pltpu.VMEM((NZ, 16, 384), F32),
             pltpu.VMEM((NZ, 16, 128), F32),
@@ -422,7 +456,6 @@
             pltpu.VMEM((16, 128), F32),
             pltpu.VMEM((16, 384), F32),
             pltpu.VMEM((4, SIDE, 512), F32),
-            pltpu.VMEM((1, 128), jnp.int32),
             pltpu.VMEM((2, 512, 128), F32),
             pltpu.VMEM((128, 128), F32),
             pltpu.VMEM((128, 128), F32),
@@ -435,13 +468,15 @@
             dma((NZ,)), dma((NZ,)), dma((NZ,)), dma((NZ,)),
             dma(()), dma((RNG,)), dma(()), dma((RNG,)), dma((RNG,)), dma(()),
         ],
-        compiler_params=pltpu.CompilerParams(collective_id=0, has_side_effects=True, vmem_limit_bytes=48 << 20),
+        compiler_params=pltpu.CompilerParams(collective_id=0, has_side_effects=True, vmem_limit_bytes=62 << 20),
         cost_estimate=pl.CostEstimate(flops=10**9, bytes_accessed=10**7, transcendentals=0),
-    )(cube, gates, looks)
+    )(cube, indices)
 
 
 def on_device(radar_cube, train_gates, look_angles):
-    return beams(radar_cube, train_gates, look_angles)[:, None]
+    indices = jnp.concatenate([
+        jnp.pad(train_gates, ((0, 0), (0, 128 - TR))), jnp.pad(look_angles, ((0, 0), (0, 128 - BEAMS)))], 0)
+    return beams(radar_cube, indices)[:, None]
 
 
 def solution(mesh):

time: 102 us -> 95.6 us (0.937)
  Pallas kernels: 99.1 us -> 92.9 us
  local copies, waits for them, and re-layouts: 3.13 us -> 1.3 us
  other arithmetic: 0 us -> 1.24 us
    pallas_call x1, Pallas kernels: 99.1 us -> 92.9 us  [beams(): pl.pallas_call(beam_kernel, out_shape=jax.ShapeDtypeStruct((2, BEAMS, 64)...]
    unnamed x7 -> x1, local copies, waits for them, and re-layouts: 3.13 us -> 1.3 us
    concatenate x0 -> x1, other arithmetic: none -> 1.24 us  [on_device(): jnp.concatenate([jnp.pad(train_gates, ((0, 0), (0, 128 - TR))), jnp.pad(l...]
where the time goes in v3:
time: 95.6 us; the launch traced here: 95.4 us
  Pallas kernels  92.9 us (97%)
  local copies, waits for them, and re-layouts  1.3 us (1%)
  other arithmetic  1.24 us (1%)
    pallas_call x1, Pallas kernels, beams(): pl.pallas_call(beam_kernel, out_shape=jax.ShapeDtypeStruct((2, BEAMS, 64)...  92.9 us

profile of v3, /device:TPU:1, one launch (start us, length us, event | category | flops | bytes accessed | tf_op | source)
XLA Modules:
  0.0 95.4 jit_solution(9643501077629305320)
XLA Ops:
  0.0 1.2 %pad_add_fusion.indices = s32[2,128]{1,0:T(2,128)} fusion(s32[1,8]{1,0:T(1,128)} %param.5, s32[1,48]{1,0:T(1,128)} %param.4), kind=kLoop, calls=%fused_computation | loop fusion | flops 256 | bytes 1248 | tf_op jit(solution)/shard_map/concatenate | solution.py:477
  1.2 92.9 %shard_map.37 = f32[2,8,64]{2,1,0:T(8,128)} custom-call(bf16[2,8,64,512]{3,2,1,0:T(8,128)(2,1)} %cube.1, s32[2,128]{1,0:T(2,128)} %pad_add_fusion.indices), custom_call_target="tpu_custom_call" | custom-call | flops 1000000000 | bytes 10000000 | tf_op jit(solution)/shard_map/pallas_call | solution.py:439
  94.1 1.3 %copy.6 = f32[2,1,8,64]{3,2,1,0:T(8,128)} copy(f32[2,1,8,64]{3,2,1,0:T(8,128)} %bitcast.3) | data formatting | bytes 8192

commit v4 on v3

--- a/solution.py
+++ b/solution.py
@@ -21,7 +21,6 @@
 NX = 4
 NZ = 8
 RNG = NX * NZ
-SIDE = 128
 TR = 48
 TRAIN = 1536
 ROOTS = (0, 20)
@@ -110,24 +109,16 @@
             rr, ri = ahead_r, ahead_i
 
 
-def beam_kernel(cube, indices, out, got, send, even, odd, raw, spec, rows, part_d, part_r, share_d, share_r,
-                sum_d, sum_r, full, steer, dr, di, row, w, x_ref, weights,
-                own_sem, a_send, a_recv, b_send, b_recv, x_send, x_recv, rd_send, rd_recv, rr_send, rr_recv,
-                gd_send, gd_recv, gr_send, gr_recv, w_send, w_recv):
+def beam_kernel(cube, indices, out, got, send, even, odd, raw, spec, rows, stat, stats, big, steer, dr, di, row, w,
+                emb, s_ref, y_ref, x_ref, weights,
+                own_sem, a_send, a_recv, b_send, b_recv, t_send, t_recv, g_send, g_recv, w_send, w_recv):
     dop = lax.axis_index("dop")
     rng = lax.axis_index("rng")
-    x, z = rng // NZ, lax.rem(rng, NZ)
     root = jnp.where(lax.rem(dop, 2) == 0, ROOTS[0], ROOTS[1])
     is_root = rng == root
 
     def dop_peer(step):
         return {"dop": lax.rem(dop + step, DOP)}
-
-    def x_peer(step):
-        return {"rng": lax.rem(x + step, NX) * NZ + z}
-
-    def z_peer(step):
-        return {"rng": x * NZ + lax.rem(z + step, NZ)}
 
     def loop(count, body, start=1):
         def one(step, carry):
@@ -154,23 +145,16 @@
         pl.semaphore_signal(barrier, inc=1, device_id=peer, device_id_type=MESH)
 
     loop(DOP, lambda step: greet(dop_peer(step)))
-    aside = (root // NZ != x) & (lax.rem(root, NZ) != z)
 
     @pl.when(is_root)
     def _():
-        loop(RNG, lambda step: greet({"rng": lax.rem(rng + step, RNG)}))
+        others(lambda r: greet({"rng": r}))
 
     @pl.when(jnp.logical_not(is_root))
     def _():
-        loop(NX, lambda step: greet(x_peer(step)))
-        loop(NZ, lambda step: greet(z_peer(step)))
-
-    @pl.when(aside)
-    def _():
         greet({"rng": root})
 
-    near_count = DOP + NX + NZ - 3
-    pl.semaphore_wait(barrier, jnp.where(is_root, DOP + RNG - 2, jnp.where(aside, near_count + 1, near_count)))
+    pl.semaphore_wait(barrier, jnp.where(is_root, DOP + RNG - 2, DOP))
 
     def tile_of(index):
         return (pl.ds(pl.multiple_of(index // 4 * 16, 16), 16),
@@ -244,80 +228,32 @@
     spec[:, g, c] = send[dop]
     loop(DOP, lambda step: b_copy(step).wait_recv())
 
-    for i in range(2):
-        rows[0, i] = lax.dot_general(
-            pick, spec[i], (((0,), (0,)), ((), ())), preferred_element_type=F32).astype(BF16)
-
-    def x_copy(step):
+    squares = jnp.zeros((8, 128), F32)
+    for j in range(4):
+        for i in range(2):
+            chosen = lax.dot_general(
+                pick, spec[i, :, 128*j:128*j+128], (((0,), (0,)), ((), ())), preferred_element_type=F32)
+            rows[j, :, 128*i:128*i+128] = chosen.astype(BF16)
+            for e in range(0, TR, 8):
+                squares = squares + chosen[e:e+8] * chosen[e:e+8]
+    stat[...] = squares
+
+    def g_copy(j, r, target):
         return pltpu.make_async_remote_copy(
-            src_ref=rows.at[0], dst_ref=rows.at[step], send_sem=x_send.at[step],
-            recv_sem=x_recv.at[step], device_id=x_peer(step), device_id_type=MESH)
-
-    far_first(NX, lambda step: x_copy(step).start())
-    loop(NX, lambda step: x_copy(step).wait_recv())
-
-    def columns(block):
-        at = pl.ds(pl.multiple_of(block * SIDE, SIDE), SIDE)
-        return (rows[:, 0, :, at].reshape(NX * TR, SIDE), rows[:, 1, :, at].reshape(NX * TR, SIDE))
-
-    def dot(a, b):
-        return lax.dot_general(a, b, (((0,), (0,)), ((), ())), preferred_element_type=F32)
-
-    def power(a, b):
-        return dot(a[0], b[0]) + dot(a[1], b[1])
-
-    def cross(a, b):
-        return dot(a[0], b[1]) - dot(a[1], b[0])
-
-    def r_copy(part, share, sends, recvs, step):
+            src_ref=rows.at[j], dst_ref=big.at[j, r], send_sem=g_send.at[j], recv_sem=g_recv.at[j, r],
+            device_id={"rng": target}, device_id_type=MESH)
+
+    def t_copy(r, target):
         return pltpu.make_async_remote_copy(
-            src_ref=part.at[lax.rem(z + step, NZ)], dst_ref=share.at[step], send_sem=sends.at[step],
-            recv_sem=recvs.at[step], device_id=z_peer(step), device_id_type=MESH)
-
-    rd_copy = functools.partial(r_copy, part_d, share_d, rd_send, rd_recv)
-    rr_copy = functools.partial(r_copy, part_r, share_r, rr_send, rr_recv)
-    mine = columns(x)
-    eye = lax.broadcasted_iota(jnp.int32, (SIDE, SIDE), 0) - lax.broadcasted_iota(jnp.int32, (SIDE, SIDE), 1)
-    part_d[...] = jnp.where(eye >= 0, power(mine, mine), cross(mine, mine)).reshape(NZ, 16, SIDE)
-    far_first(NZ, lambda step: rd_copy(step).start())
-    near, far = lax.rem(x + 1, NX), lax.rem(x + 2, NX)
-    low1, high1 = columns(jnp.minimum(x, near)), columns(jnp.maximum(x, near))
-    low2, high2 = columns(jnp.minimum(x, far)), columns(jnp.maximum(x, far))
-    part_r[:, :, 0:128] = power(low1, high1).reshape(NZ, 16, SIDE)
-    part_r[:, :, 128:256] = cross(low1, high1).reshape(NZ, 16, SIDE)
-    part_r[:, :, 256:384] = jnp.where(x < 2, power(low2, high2), cross(low2, high2)).reshape(NZ, 16, SIDE)
-    far_first(NZ, lambda step: rr_copy(step).start())
-
-    strip = pl.ds(pl.multiple_of(z * 16, 16), 16)
-
-    def strip_of(r, at):
-        return full.at[r // NZ, pl.ds(pl.multiple_of(lax.rem(r, NZ) * 16, 16), 16), at]
-
-    def gd_copy(r, target):
-        return pltpu.make_async_remote_copy(
-            src_ref=sum_d, dst_ref=strip_of(r, slice(0, 128)), send_sem=gd_send, recv_sem=gd_recv.at[r],
+            src_ref=stat, dst_ref=stats.at[r], send_sem=t_send, recv_sem=t_recv.at[r],
             device_id={"rng": target}, device_id_type=MESH)
 
-    def gr_copy(r, target):
-        return pltpu.make_async_remote_copy(
-            src_ref=sum_r, dst_ref=strip_of(r, slice(128, 512)), send_sem=gr_send, recv_sem=gr_recv.at[r],
-            device_id={"rng": target}, device_id_type=MESH)
-
-    def total(part, share, copy):
-        loop(NZ, lambda step: copy(step).wait_recv())
-        value = part[z]
-        for step in range(1, NZ):
-            value = value + share[step]
-        return value * (1.0 / TRAIN)
-
-    value_d = total(part_d, share_d, rd_copy)
-
     @pl.when(jnp.logical_not(is_root))
     def _():
-        sum_d[...] = value_d
-        gd_copy(rng, root).start()
-        sum_r[...] = total(part_r, share_r, rr_copy)
-        gr_copy(rng, root).start()
+        g_copy(0, rng, root).start()
+        t_copy(rng, root).start()
+        for j in range(1, 4):
+            g_copy(j, rng, root).start()
 
     def w_copy(r):
         return pltpu.make_async_remote_copy(
@@ -326,30 +262,19 @@
 
     @pl.when(is_root)
     def _():
-        full[x, strip, 0:128] = value_d
-        others(lambda r: gd_copy(r, root).wait_recv())
-        trace = jnp.zeros((), F32)
-        for i in range(4):
-            trace = trace + jnp.sum(jnp.where(eye == 0, full[i, :, 0:128], 0.0))
-        load = LOAD * trace / 512.0
-        for i in range(4):
-            t = full[i, :, 0:128]
-            tt = t.T
-            row[i, 0:128, 128*i:128*i+128] = jnp.where(eye > 0, t, tt) + jnp.where(eye == 0, load, 0.0)
-            row[i, 128:256, 128*i:128*i+128] = jnp.where(eye > 0, tt, jnp.where(eye < 0, -t, 0.0))
-            row[i, 0:128, 512:640] = steer[0, 128*i:128*i+128, :]
-            row[i, 128:256, 512:640] = steer[1, 128*i:128*i+128, :]
-
-        def rest():
-            full[x, strip, 128:512] = total(part_r, share_r, rr_copy)
-            others(lambda r: gr_copy(r, root).wait_recv())
-            for i in range(4):
-                for j in range(i + 1, 4):
-                    (a, b), (e, d) = place(i, j)
-                    row[i, 0:128, 128*j:128*j+128] = full[a, :, 128*b:128*b+128]
-                    row[i, 128:256, 128*j:128*j+128] = -full[e, :, 128*d:128*d+128]
-
-        solve(rest, steer, row, w, x_ref, dr, di, weights)
+        stats[rng] = squares
+        for j in range(4):
+            big[j, rng] = rows[j]
+        others(lambda r: t_copy(r, root).wait_recv())
+        load = jnp.sum(jnp.sum(stats[...], axis=0)) * (LOAD / (512.0 * TRAIN))
+        for k in range(4):
+            top, low = steer[0, 128*k:128*k+128, :], steer[1, 128*k:128*k+128, :]
+            s_ref[k] = jnp.concatenate([top, low], 0)
+
+        def arrive(j):
+            others(lambda r: g_copy(j, r, root).wait_recv())
+
+        solve(arrive, load, big, steer, s_ref, row, w, emb, y_ref, x_ref, dr, di, weights)
         others(lambda r: w_copy(r).start())
 
     @pl.when(jnp.logical_not(is_root))
@@ -368,62 +293,83 @@
 
     @pl.when(jnp.logical_not(is_root))
     def _():
-        gd_copy(rng, root).wait_send()
-        gr_copy(rng, root).wait_send()
+        t_copy(rng, root).wait_send()
+        for j in range(4):
+            g_copy(j, rng, root).wait_send()
 
     loop(DOP, lambda step: a_copy(step).wait_send())
     loop(DOP, lambda step: b_copy(step).wait_send())
-    loop(NX, lambda step: x_copy(step).wait_send())
-    loop(NZ, lambda step: rd_copy(step).wait_send())
-    loop(NZ, lambda step: rr_copy(step).wait_send())
-
-
-def place(i, j):
-    if j - i == 1:
-        return (i, 1), (i, 2)
-    if j - i == 3:
-        return (3, 1), (3, 2)
-    return (i, 3), (i + 2, 3)
-
-
-def solve(rest, steer, row, w, x, dr, di, weights):
+
+
+def companion(v):
+    top, low = v[0:128], v[128:256]
+    return jnp.concatenate([jnp.concatenate([top, low], 1), jnp.concatenate([low, -top], 1)], 0)
+
+
+def solve(arrive, load, big, steer, s_ref, row, w, emb, y_ref, x, dr, di, weights):
+    diagonal = lax.broadcasted_iota(jnp.int32, (128, 128), 0) == lax.broadcasted_iota(jnp.int32, (128, 128), 1)
+    turned = (((0,), (0,)), ((), ()))
+
+    def high(a, b):
+        return jnp.dot(a, b, preferred_element_type=F32, precision=HIGH)
+
+    def high_turned(a, b):
+        return lax.dot_general(a, b, turned, preferred_element_type=F32, precision=HIGH)
+
+    def at(k):
+        return slice(128 * k, 128 * k + 128)
+
+    def column(j):
+        arrive(j)
+        mine = big[j].reshape(TRAIN, 256)
+        for k in range(j + 1):
+            g = lax.dot_general(mine, big[k].reshape(TRAIN, 256), turned, preferred_element_type=F32)
+            power = (g[0:128, 0:128] + g[128:256, 128:256]) * (1.0 / TRAIN)
+            cross = (g[0:128, 128:256] - g[128:256, 0:128]) * (1.0 / TRAIN)
+            if k < j:
+                row[k, 0:128, at(j)] = power.T
+                row[k, 128:256, at(j)] = cross.T
+            else:
+                dr[...] = jnp.where(diagonal, power + load, power)
+                di[...] = -cross
+        for k in range(j):
+            if k > 0:
+                lhs = jnp.concatenate([row[l, :, at(k)] for l in range(k)], 0)
+                rhs = jnp.concatenate([companion(w[l, :, at(j)]) for l in range(k)], 0)
+                u = high_turned(lhs, rhs)
+                row[k, 0:128, at(j)] -= u[:, 0:128]
+                row[k, 128:256, at(j)] -= u[:, 128:256]
+            w[k, :, at(j)] = high(emb[k], row[k, :, at(j)])
+        if j > 0:
+            lhs = jnp.concatenate([row[k, :, at(j)] for k in range(j)], 0)
+            rhs = jnp.concatenate([
+                jnp.concatenate([companion(w[k, :, at(j)]), companion(y_ref[k])], 1) for k in range(j)], 0)
+            u = high_turned(lhs, rhs)
+            dr[...] -= u[:, 0:128]
+            di[...] -= u[:, 128:256]
+            s_ref[j, 0:128] -= u[:, 256:384]
+            s_ref[j, 128:256] -= u[:, 384:512]
+
     def body(k, carry):
         for kk in range(4):
             @pl.when(k == kk)
             def _():
-                dr[...] = row[kk, 0:128, 128*kk:128*kk+128]
-                di[...] = row[kk, 128:256, 128*kk:128*kk+128]
+                column(kk)
         invert_block(dr, di)
-        for kk in range(4):
-            @pl.when(k == kk)
-            def _():
-                if kk == 0:
-                    rest()
-                s = 128 * (kk + 1)
-                a, b = dr[...], di[...]
-                emb = jnp.concatenate([jnp.concatenate([a, -b], 1), jnp.concatenate([b, a], 1)], 0)
-                w[kk, :, s:640] = jnp.dot(emb, row[kk, :, s:640], preferred_element_type=F32, precision=HIGH)
-                for i in range(kk + 1, 4):
-                    c = 128 * i
-                    lhs = row[kk, :, c:c+128]
-                    wr = w[kk, 0:128, c:640]
-                    wi = w[kk, 128:256, c:640]
-                    both = jnp.concatenate([jnp.concatenate([wr, wi], 1), jnp.concatenate([wi, -wr], 1)], 0)
-                    n = 640 - c
-                    u = lax.dot_general(lhs, both, (((0,), (0,)), ((), ())), preferred_element_type=F32, precision=HIGH)
-                    row[i, 0:128, c:640] -= u[:, :n]
-                    row[i, 128:256, c:640] -= u[:, n:]
+        a, b = dr[...], di[...]
+        emb[k] = jnp.concatenate([jnp.concatenate([a, -b], 1), jnp.concatenate([b, a], 1)], 0)
+        y_ref[k] = high(emb[k], s_ref[k])
         return carry
 
     lax.fori_loop(0, 4, body, 0)
     q = jnp.zeros((1, 128), F32)
     for k in (3, 2, 1, 0):
-        y = w[k, :, 512:640]
+        y = y_ref[k]
         for j in range(k + 1, 4):
             wr = w[k, 0:128, 128*j:128*j+128]
             wi = w[k, 128:256, 128*j:128*j+128]
-            emb = jnp.concatenate([jnp.concatenate([wr, -wi], 1), jnp.concatenate([wi, wr], 1)], 0)
-            y = y - jnp.dot(emb, x[j], preferred_element_type=F32, precision=HIGH)
+            full = jnp.concatenate([jnp.concatenate([wr, -wi], 1), jnp.concatenate([wi, wr], 1)], 0)
+            y = y - jnp.dot(full, x[j], preferred_element_type=F32, precision=HIGH)
         x[k] = y
         for h in range(2):
             q = q + jnp.sum(y[128*h:128*h+128] * steer[h, 128*k:128*k+128, :], axis=0, keepdims=True)
@@ -448,27 +394,25 @@
             pltpu.VMEM((2, 8, 16, 128), F32),
             pltpu.VMEM((DOP, 2, 16, 128), F32),
             pltpu.VMEM((2, 64, 512), BF16),
-            pltpu.VMEM((NX, 2, TR, 512), BF16),
-            pltpu.VMEM((NZ, 16, 128), F32),
-            pltpu.VMEM((NZ, 16, 384), F32),
-            pltpu.VMEM((NZ, 16, 128), F32),
-            pltpu.VMEM((NZ, 16, 384), F32),
-            pltpu.VMEM((16, 128), F32),
-            pltpu.VMEM((16, 384), F32),
-            pltpu.VMEM((4, SIDE, 512), F32),
+            pltpu.VMEM((4, TR, 256), BF16),
+            pltpu.VMEM((8, 128), F32),
+            pltpu.VMEM((RNG, 8, 128), F32),
+            pltpu.VMEM((4, RNG, TR, 256), BF16),
             pltpu.VMEM((2, 512, 128), F32),
             pltpu.VMEM((128, 128), F32),
             pltpu.VMEM((128, 128), F32),
-            pltpu.VMEM((4, 256, 640), F32),
-            pltpu.VMEM((4, 256, 640), F32),
+            pltpu.VMEM((4, 256, 512), F32),
+            pltpu.VMEM((4, 256, 512), F32),
+            pltpu.VMEM((4, 256, 256), F32),
+            pltpu.VMEM((4, 256, 128), F32),
+            pltpu.VMEM((4, 256, 128), F32),
             pltpu.VMEM((4, 256, 128), F32),
             pltpu.VMEM((16, 512), BF16),
             dma(()),
-            dma((DOP,)), dma((DOP,)), dma((DOP,)), dma((DOP,)), dma((NX,)), dma((NX,)),
-            dma((NZ,)), dma((NZ,)), dma((NZ,)), dma((NZ,)),
-            dma(()), dma((RNG,)), dma(()), dma((RNG,)), dma((RNG,)), dma(()),
+            dma((DOP,)), dma((DOP,)), dma((DOP,)), dma((DOP,)),
+            dma(()), dma((RNG,)), dma((4,)), dma((4, RNG)), dma((RNG,)), dma(()),
         ],
-        compiler_params=pltpu.CompilerParams(collective_id=0, has_side_effects=True, vmem_limit_bytes=62 << 20),
+        compiler_params=pltpu.CompilerParams(collective_id=0, has_side_effects=True, vmem_limit_bytes=53 << 20),
         cost_estimate=pl.CostEstimate(flops=10**9, bytes_accessed=10**7, transcendentals=0),
     )(cube, indices)
 

time: 95.6 us -> 96.5 us (level)
  Pallas kernels: 92.9 us -> 95.1 us
    pallas_call x1, Pallas kernels: 92.9 us -> 95.1 us  [beams(): pl.pallas_call(beam_kernel, out_shape=jax.ShapeDtypeStruct((2, BEAMS, 64)...]
where the time goes in v4:
time: 96.5 us; the launch traced here: 96.4 us
  Pallas kernels  95.1 us (99%)
    pallas_call x1, Pallas kernels, beams(): pl.pallas_call(beam_kernel, out_shape=jax.ShapeDtypeStruct((2, BEAMS, 64)...  95.1 us

profile of v4, /device:TPU:1, one launch (start us, length us, event | category | flops | bytes accessed | tf_op | source)
XLA Modules:
  0.0 96.4 jit_solution(3678562259244925834)
XLA Ops:
  0.0 0.7 pad_add_fusion.indices
  0.7 95.1 %shard_map.37 = f32[2,8,64]{2,1,0:T(8,128)S(1)} custom-call(bf16[2,8,64,512]{3,2,1,0:T(8,128)(2,1)} %cube.1, s32[2,128]{1,0:T(2,128)S(1)} %pad_add_fusion.indices), custom_call_target="tpu_custom_call" | custom-call | flops 1000000000 | bytes 10000000 | tf_op jit(solution)/shard_map/pallas_call | solution.py:385
  95.8 0.6 copy.6

commit v5 on v3

--- a/solution.py
+++ b/solution.py
@@ -468,7 +468,7 @@
             dma((NZ,)), dma((NZ,)), dma((NZ,)), dma((NZ,)),
             dma(()), dma((RNG,)), dma(()), dma((RNG,)), dma((RNG,)), dma(()),
         ],
-        compiler_params=pltpu.CompilerParams(collective_id=0, has_side_effects=True, vmem_limit_bytes=62 << 20),
+        compiler_params=pltpu.CompilerParams(collective_id=0, has_side_effects=True, vmem_limit_bytes=53 << 20),
         cost_estimate=pl.CostEstimate(flops=10**9, bytes_accessed=10**7, transcendentals=0),
     )(cube, indices)
 

time: 95.6 us -> 92.7 us (0.970)
  Pallas kernels: 92.9 us -> 91.3 us
    pallas_call x1, Pallas kernels: 92.9 us -> 91.3 us  [beams(): pl.pallas_call(beam_kernel, out_shape=jax.ShapeDtypeStruct((2, BEAMS, 64)...]
where the time goes in v5:
time: 92.7 us; the launch traced here: 92.6 us
  Pallas kernels  91.3 us (98%)
    pallas_call x1, Pallas kernels, beams(): pl.pallas_call(beam_kernel, out_shape=jax.ShapeDtypeStruct((2, BEAMS, 64)...  91.3 us

profile of v5, /device:TPU:1, one launch (start us, length us, event | category | flops | bytes accessed | tf_op | source)
XLA Modules:
  0.0 92.6 jit_solution(13705161779534765639)
XLA Ops:
  0.0 0.7 pad_add_fusion.indices
  0.7 91.3 %shard_map.37 = f32[2,8,64]{2,1,0:T(8,128)S(1)} custom-call(bf16[2,8,64,512]{3,2,1,0:T(8,128)(2,1)} %cube.1, s32[2,128]{1,0:T(2,128)S(1)} %pad_add_fusion.indices), custom_call_target="tpu_custom_call" | custom-call | flops 1000000000 | bytes 10000000 | tf_op jit(solution)/shard_map/pallas_call | solution.py:439
  92.0 0.6 copy.6

commit v6 on v5

--- a/solution.py
+++ b/solution.py
@@ -24,7 +24,7 @@
 SIDE = 128
 TR = 48
 TRAIN = 1536
-ROOTS = (0, 20)
+ROOTS = (0, 16)
 
 
 def twiddles():
@@ -142,7 +142,9 @@
         loop(count, one)
 
     def others(body):
-        def one(r):
+        def one(i):
+            r = lax.rem(i, NX) * NZ + i // NX
+
             @pl.when(r != rng)
             def _():
                 body(r)
@@ -419,11 +421,12 @@
     q = jnp.zeros((1, 128), F32)
     for k in (3, 2, 1, 0):
         y = w[k, :, 512:640]
-        for j in range(k + 1, 4):
-            wr = w[k, 0:128, 128*j:128*j+128]
-            wi = w[k, 128:256, 128*j:128*j+128]
-            emb = jnp.concatenate([jnp.concatenate([wr, -wi], 1), jnp.concatenate([wi, wr], 1)], 0)
-            y = y - jnp.dot(emb, x[j], preferred_element_type=F32, precision=HIGH)
+        if k < 3:
+            known = jnp.concatenate([
+                jnp.concatenate([x[j, 0:128], x[j, 128:256]], 1) for j in range(k + 1, 4)], 0)
+            u = jnp.dot(w[k, :, 128*k+128:512], known, preferred_element_type=F32, precision=HIGH)
+            y = y - jnp.concatenate([
+                u[0:128, 0:128] - u[128:256, 128:256], u[128:256, 0:128] + u[0:128, 128:256]], 0)
         x[k] = y
         for h in range(2):
             q = q + jnp.sum(y[128*h:128*h+128] * steer[h, 128*k:128*k+128, :], axis=0, keepdims=True)

time: 92.7 us -> 91.2 us (0.984); the launches traced: 92.6 us -> 90 us
  Pallas kernels: 91.3 us -> 88.8 us
    pallas_call x1, Pallas kernels: 91.3 us -> 88.8 us  [beams(): pl.pallas_call(beam_kernel, out_shape=jax.ShapeDtypeStruct((2, BEAMS, 64)...]
where the time goes in v6:
time: 91.2 us; the launch traced here: 90 us
  Pallas kernels  88.8 us (97%)
    pallas_call x1, Pallas kernels, beams(): pl.pallas_call(beam_kernel, out_shape=jax.ShapeDtypeStruct((2, BEAMS, 64)...  88.8 us

profile of v6, /device:TPU:1, one launch (start us, length us, event | category | flops | bytes accessed | tf_op | source)
XLA Modules:
  0.0 90.0 jit_solution(13744946064723708471)
XLA Ops:
  0.0 0.7 pad_add_fusion.indices
  0.7 88.8 %shard_map.37 = f32[2,8,64]{2,1,0:T(8,128)S(1)} custom-call(bf16[2,8,64,512]{3,2,1,0:T(8,128)(2,1)} %cube.1, s32[2,128]{1,0:T(2,128)S(1)} %pad_add_fusion.indices), custom_call_target="tpu_custom_call" | custom-call | flops 1000000000 | bytes 10000000 | tf_op jit(solution)/shard_map/pallas_call | solution.py:442
  89.4 0.6 copy.6

commit v7 on v6

--- a/solution.py
+++ b/solution.py
@@ -321,6 +321,15 @@
         sum_r[...] = total(part_r, share_r, rr_copy)
         gr_copy(rng, root).start()
 
+    before = lax.rem(root + NZ - 1, NZ)
+    relays = z == before
+
+    def along_x(step):
+        return lax.rem(x + step, NX) * NZ + z
+
+    def along_z(step):
+        return x * NZ + lax.rem(z + step, NZ)
+
     def w_copy(r):
         return pltpu.make_async_remote_copy(
             src_ref=weights, dst_ref=weights, send_sem=w_send.at[r], recv_sem=w_recv,
@@ -352,11 +361,17 @@
                     row[i, 128:256, 128*j:128*j+128] = -full[e, :, 128*d:128*d+128]
 
         solve(rest, steer, row, w, x_ref, dr, di, weights)
-        others(lambda r: w_copy(r).start())
+        loop(NX, lambda step: w_copy(along_x(step)).start())
+        for ahead in (1, NZ - 1, 2):
+            loop(NX, lambda column: w_copy(column * NZ + lax.rem(root + ahead, NZ)).start(), 0)
 
     @pl.when(jnp.logical_not(is_root))
     def _():
         w_copy(root).wait_recv()
+
+    @pl.when(relays)
+    def _():
+        loop(NZ, lambda step: w_copy(along_z(step)).start(), 4)
 
     across = (((1,), (1,)), ((), ()))
     with_re = lax.dot_general(weights[...], spec[0], across, preferred_element_type=F32)
@@ -366,7 +381,13 @@
 
     @pl.when(is_root)
     def _():
-        others(lambda r: w_copy(r).wait_send())
+        loop(NX, lambda step: w_copy(along_x(step)).wait_send())
+        for ahead in (1, NZ - 1, 2):
+            loop(NX, lambda column: w_copy(column * NZ + lax.rem(root + ahead, NZ)).wait_send(), 0)
+
+    @pl.when(relays)
+    def _():
+        loop(NZ, lambda step: w_copy(along_z(step)).wait_send(), 4)
 
     @pl.when(jnp.logical_not(is_root))
     def _():

time: 91.2 us -> 92.2 us (1.011)
  the two profiles are of different devices: /device:TPU:1 before, /device:TPU:198 now
where the time goes in v7:
time: 92.2 us; the launch traced here: 92.1 us
  Pallas kernels  90.8 us (98%)
    pallas_call x1, Pallas kernels, beams(): pl.pallas_call(beam_kernel, out_shape=jax.ShapeDtypeStruct((2, BEAMS, 64)...  90.8 us

profile of v7, /device:TPU:198, one launch (start us, length us, event | category | flops | bytes accessed | tf_op | source)
XLA Modules:
  0.0 92.1 jit_solution(10104765586411235207)
XLA Ops:
  0.0 0.7 pad_add_fusion.indices
  0.7 90.8 %shard_map.37 = f32[2,8,64]{2,1,0:T(8,128)S(1)} custom-call(bf16[2,8,64,512]{3,2,1,0:T(8,128)(2,1)} %cube.1, s32[2,128]{1,0:T(2,128)S(1)} %pad_add_fusion.indices), custom_call_target="tpu_custom_call" | custom-call | flops 1000000000 | bytes 10000000 | tf_op jit(solution)/shard_map/pallas_call | solution.py:463
  91.5 0.6 copy.6

commit v8 on v6

--- a/solution.py
+++ b/solution.py
@@ -197,6 +197,8 @@
         phase = turn.astype(F32) * (math.pi / NANG)
         steer[0, 128*k:128*k+128, :] = jnp.where(lanes < BEAMS, jnp.cos(phase), 0.0)
         steer[1, 128*k:128*k+128, :] = jnp.where(lanes < BEAMS, jnp.sin(phase), 0.0)
+        row[k, 0:128, 512:640] = steer[0, 128*k:128*k+128, :]
+        row[k, 128:256, 512:640] = steer[1, 128*k:128*k+128, :]
     gate = lax.broadcasted_iota(jnp.int32, (64, TR), 0)
     pick = jnp.where(gate == indices[0:1, 0:TR], 1.0, 0.0).astype(BF16)
 
@@ -339,8 +341,6 @@
             tt = t.T
             row[i, 0:128, 128*i:128*i+128] = jnp.where(eye > 0, t, tt) + jnp.where(eye == 0, load, 0.0)
             row[i, 128:256, 128*i:128*i+128] = jnp.where(eye > 0, tt, jnp.where(eye < 0, -t, 0.0))
-            row[i, 0:128, 512:640] = steer[0, 128*i:128*i+128, :]
-            row[i, 128:256, 512:640] = steer[1, 128*i:128*i+128, :]
 
         def rest():
             full[x, strip, 128:512] = total(part_r, share_r, rr_copy)

time: 91.2 us -> 91.2 us (level)
  no operation moved by 1% of the time
where the time goes in v8:
time: 91.2 us; the launch traced here: 90 us
  Pallas kernels  88.7 us (97%)
    pallas_call x1, Pallas kernels, beams(): pl.pallas_call(beam_kernel, out_shape=jax.ShapeDtypeStruct((2, BEAMS, 64)...  88.7 us

profile of v8, /device:TPU:1, one launch (start us, length us, event | category | flops | bytes accessed | tf_op | source)
XLA Modules:
  0.0 90.0 jit_solution(9017604719817866369)
XLA Ops:
  0.0 0.7 pad_add_fusion.indices
  0.7 88.7 %shard_map.37 = f32[2,8,64]{2,1,0:T(8,128)S(1)} custom-call(bf16[2,8,64,512]{3,2,1,0:T(8,128)(2,1)} %cube.1, s32[2,128]{1,0:T(2,128)S(1)} %pad_add_fusion.indices), custom_call_target="tpu_custom_call" | custom-call | flops 1000000000 | bytes 10000000 | tf_op jit(solution)/shard_map/pallas_call | solution.py:442
  89.4 0.6 copy.6
